TPU v7x, 512 devices: a whole 4x4x16 slice. The times are simulated.
512 devices in a mesh: img: 64 (over x, z_lo, core), blk: 8 (over z_hi, y).
Axes of the slice: x: 4, y: 4, z: 16 (z_hi: 2, z_lo: 8; z = z_hi * 8 + z_lo), core: 2. Of those that a mesh axis runs over, the one named last changes fastest.
Arguments:
- image_embeds: bfloat16 [6144, 1152], P(('img', 'blk')), may hold values from -48 to 48
- text_embeds: bfloat16 [6144, 1152], P(('img', 'blk')), may hold values from -48 to 48
- log_temp: float32 [1], replicated, may hold values from 1 to 2.3
- bias: float32 [1], replicated, may hold values from -3 to -1
Outputs:
- image_grads: float32 [6144, 1152], P(('img', 'blk'))
- text_grads: float32 [6144, 1152], P(('img', 'blk'))
All inputs are finite; a program needn't handle non-finite values.
Results may differ from a plain program's by a relative error of at most 0.00145.
Values may be sent and summed in bfloat16 or wider, within the bound.
No kernel may reach another device: no remote copies, remote signals or barrier semaphores. Data moves between devices by JAX's collectives and lax.ppermute only.
A program may use at most 64 MiB of HBM per device.

v0:
```python
import jax
import jax.numpy as jnp
from jax import lax
from jax.experimental import pallas as pl
from jax.experimental.pallas import tpu as pltpu
from jax.sharding import Mesh, PartitionSpec as P

EPS = 1e-06
AXES = ("x", "zm", "zn", "core", "zh", "y")
SIZES = (4, 2, 4, 2, 2, 4)
PLANE = ("x", "core", "y")
LINE = ("zm", "zn", "zh")
FAR = (0, 4, 12, 8)
VMEM = 48 * 1024 * 1024

ROWS = 12
WIDTH = 1152
TALL = 16
MAIN = 896
REST = WIDTH - MAIN
STEP = TALL - ROWS
PIECES = [
    (
        slice(m * STEP, (m + 1) * STEP),
        slice(g * 128, (g + 1) * 128),
        slice((3 * g + m) * 128, (3 * g + m + 1) * 128),
    )
    for g in range(REST // 128)
    for m in range(ROWS // STEP)
]


def unit_rows(emb):
    wide = emb.astype(jnp.float32)
    inverse = lax.rsqrt(jnp.sum(wide * wide, axis=1, keepdims=True) + EPS)
    return (wide * inverse, inverse)


def spread_kernel(emb_ref, out_ref, block):
    unit, _ = unit_rows(emb_ref[...])
    block[:ROWS, :] = unit[:, :MAIN]
    block[ROWS:, :] = jnp.zeros((STEP, MAIN), jnp.float32)
    for rows, cols, place in PIECES:
        block[ROWS:, place] = unit[rows, MAIN + cols.start : MAIN + cols.stop]
    out_ref[...] = jnp.broadcast_to(block[...].astype(jnp.bfloat16)[None], out_ref.shape)


def spread(emb, peers):
    return pl.pallas_call(
        spread_kernel,
        out_shape=jax.ShapeDtypeStruct((peers, TALL, MAIN), jnp.bfloat16),
        scratch_shapes=[pltpu.VMEM((TALL, MAIN), jnp.float32)],
        compiler_params=pltpu.CompilerParams(vmem_limit_bytes=VMEM),
        cost_estimate=pl.CostEstimate(flops=100_000, bytes_accessed=1_000_000, transcendentals=0),
    )(emb)


def pair_kernel(temp_ref, bias_ref, place_ref, images_ref, *refs):
    text_refs = refs[:4]
    core_out, image_out, text_out = refs[4:7]
    images, texts, rest, main = refs[7:]
    n_images = images_ref.shape[0]
    far = text_refs[0].shape[0]
    groups = [(images, 0, images_ref)]
    groups += [(texts, i * far, ref) for i, ref in enumerate(text_refs)]
    rest[:, ROWS:, :] = jnp.zeros((n_images, STEP, REST), jnp.float32)
    for whole, first, ref in groups:
        n = ref.shape[0]
        span = pl.ds(first * TALL, n * TALL)
        whole[span, :MAIN] = ref[...].reshape(n * TALL, MAIN)
        for rows, cols, place in PIECES:
            rest[:n, rows, cols] = ref[:, ROWS:, place].astype(jnp.float32)
        whole[span, MAIN:] = rest[:n].reshape(n * TALL, REST).astype(jnp.bfloat16)

    scale = jnp.exp(jnp.full((1, 1), temp_ref[0], jnp.float32))
    logits = (
        scale
        * lax.dot_general(
            images[...], texts[...], (((1,), (1,)), ((), ())), preferred_element_type=jnp.float32
        )
        + bias_ref[0]
    )
    x, core, y, z = (place_ref[i] for i in range(4))
    row = lax.broadcasted_iota(jnp.int32, logits.shape, 0)
    col = lax.broadcasted_iota(jnp.int32, logits.shape, 1)
    row_in, col_in = row % TALL, col % TALL
    real = (row_in < ROWS) & (col_in < ROWS)
    same = (row == col + (x * 8 + core * 4 + y) * TALL) & (col < TALL)
    sig = jax.nn.sigmoid(jnp.where(same, -logits, logits))
    coeff = jnp.where(real, jnp.where(same, -sig, sig) * scale, 0.0).astype(jnp.bfloat16)

    def pack(n):
        for rows, cols, place in PIECES:
            main[:n, ROWS:, place] = rest[:n, rows, cols]

    main[...] = jnp.dot(
        coeff, texts[:, :MAIN], preferred_element_type=jnp.float32
    ).reshape(n_images, TALL, MAIN)
    rest[...] = jnp.dot(
        coeff, texts[:, MAIN:], preferred_element_type=jnp.float32
    ).reshape(n_images, TALL, REST)
    pack(n_images)
    for dy in range(4):
        for dx in range(4):
            spot = (x + dx) % 4 * 8 + (y + dy) % 4
            core_out[dy * 4 + dx] = main[spot + (1 - core) * 4].astype(jnp.bfloat16)
            image_out[dy * 4 + dx] = main[spot + core * 4]

    n = 4 * far
    flip = (((0,), (0,)), ((), ()))
    main[:n] = lax.dot_general(
        coeff, images[:, :MAIN], flip, preferred_element_type=jnp.float32
    ).reshape(n, TALL, MAIN)
    rest[:n] = lax.dot_general(
        coeff, images[:, MAIN:], flip, preferred_element_type=jnp.float32
    ).reshape(n, TALL, REST)
    pack(n)
    for i, near in enumerate(near_moves(z)):
        for j, by in enumerate(FAR):
            source = (z - near - by + 32) % 16
            text_out[line_place(source)] = main[i * far + j].astype(jnp.bfloat16)


def pair_terms(log_temp, bias, place, images, texts):
    n_images, n_texts = images.shape[0], 4 * texts[0].shape[0]
    return pl.pallas_call(
        pair_kernel,
        in_specs=[pl.BlockSpec(memory_space=pltpu.SMEM)] * 3
        + [pl.BlockSpec(memory_space=pltpu.VMEM)] * 5,
        out_shape=[
            jax.ShapeDtypeStruct((n_images // 2, TALL, MAIN), jnp.bfloat16),
            jax.ShapeDtypeStruct((n_images // 2, TALL, MAIN), jnp.float32),
            jax.ShapeDtypeStruct((n_texts, TALL, MAIN), jnp.bfloat16),
        ],
        scratch_shapes=[
            pltpu.VMEM((n_images * TALL, WIDTH), jnp.bfloat16),
            pltpu.VMEM((n_texts * TALL, WIDTH), jnp.bfloat16),
            pltpu.VMEM((n_images, TALL, REST), jnp.float32),
            pltpu.VMEM((n_images, TALL, MAIN), jnp.float32),
        ],
        compiler_params=pltpu.CompilerParams(vmem_limit_bytes=VMEM),
        cost_estimate=pl.CostEstimate(
            flops=900_000_000, bytes_accessed=4_000_000, transcendentals=131_072
        ),
    )(log_temp, bias, place, images, *texts)


def finish_kernel(emb_ref, back_ref, out_ref, block):
    total = jnp.sum(back_ref[...].astype(jnp.float32), axis=0)
    block[:, :MAIN] = total[:ROWS]
    for rows, cols, place in PIECES:
        block[rows, MAIN + cols.start : MAIN + cols.stop] = total[ROWS:, place]
    unit, inverse = unit_rows(emb_ref[...])
    direction = block[...]
    along = jnp.sum(unit * direction, axis=1, keepdims=True)
    out_ref[...] = (direction - unit * along) * inverse


def finish(emb, back):
    return pl.pallas_call(
        finish_kernel,
        out_shape=jax.ShapeDtypeStruct(emb.shape, jnp.float32),
        scratch_shapes=[pltpu.VMEM((ROWS, WIDTH), jnp.float32)],
        compiler_params=pltpu.CompilerParams(vmem_limit_bytes=VMEM),
        cost_estimate=pl.CostEstimate(flops=500_000, bytes_accessed=1_000_000, transcendentals=0),
    )(emb, back)


def line_place(z):
    return (z // 4 % 2) * 8 + (z % 4) * 2 + z // 8


def near_moves(z):
    return (0, 1, -1, 2 - 4 * (z % 2))


def along_z(value, move):
    pairs = [(line_place(z), line_place((z + move(z)) % 16)) for z in range(16)]
    return lax.ppermute(value, LINE, pairs)


def around(value, axis, by):
    n = lax.axis_size(axis)
    return lax.ppermute(value, axis, [(i, (i + by) % n) for i in range(n)])


def on_device(image_embeds, text_embeds, log_temp, bias):
    z = lax.axis_index("zh") * 8 + lax.axis_index("zm") * 4 + lax.axis_index("zn")
    place = jnp.stack([lax.axis_index(axis) for axis in PLANE] + [z]).astype(jnp.int32)

    images = lax.all_to_all(spread(image_embeds, lax.axis_size(PLANE)), PLANE, 0, 0)
    own = spread(text_embeds, 1)
    own = jnp.concatenate([own] + [along_z(own, lambda z, by=by: by) for by in FAR[1:]], axis=0)
    texts = [own] + [along_z(own, lambda z, i=i: near_moves(z)[i]) for i in (1, 2, 3)]

    core_part, part, text_part = pair_terms(log_temp, bias, place, images, texts)

    text_back = lax.all_to_all(text_part, LINE, 0, 0)
    part = part + around(core_part, "core", 1).astype(jnp.float32)
    part = part.reshape((4, 4) + part.shape[1:])
    part = part[0] + sum(
        around(part[by].astype(jnp.bfloat16), "y", by).astype(jnp.float32) for by in (1, 3, 2)
    )
    image_back = jnp.stack([part[0]] + [around(part[by], "x", by) for by in (1, 3, 2)], axis=0)
    return (finish(image_embeds, image_back), finish(text_embeds, text_back))


def solution(mesh):
    fine = Mesh(mesh.devices.reshape(SIZES), AXES)
    split = P(AXES, None)
    return jax.shard_map(
        on_device,
        mesh=fine,
        in_specs=(split, split, P(), P()),
        out_specs=(split, split),
        check_vma=False,
    )
```

profile of v0, /device:TPU:32, one launch (start us, length us, event | category | flops | bytes accessed | tf_op | source)
XLA Modules:
  0.0 101.2 jit_solution(1255334466186793408)
XLA Ops:
  0.6 0.0 copy-start.1
  0.6 0.8 copy-done.1
  1.4 1.1 %shard_map.59 = bf16[32,16,896]{2,1,0:T(8,128)(2,1)} custom-call(bf16[12,1152]{1,0:T(8,128)(2,1)S(1)} %copy-done.1), custom_call_target="tpu_custom_call" | custom-call | flops 100000 | bytes 1000000 | tf_op jit(solution)/shard_map/pallas_call | solution.py:49
  2.5 0.0 copy-start
  2.5 7.5 %all-to-all-start = ((bf16[32,16,896]{2,1,0:T(8,128)(2,1)}), bf16[32,16,896]{2,1,0:T(8,128)(2,1)S(1)}, u32[]{:S(2)}, u32[]{:S(2)}) async-start(bf16[32,16,896]{2,1,0:T(8,128)(2,1)} %shard_map.59), calls=%async_computation | async-start | bytes 1835008 | tf_op jit(solution)/shard_map/all_to_all | solution.py:191
  10.0 0.0 copy-done
  10.0 0.1 shard_map.60
  10.1 14.8 %collective-permute-start.2 = (bf16[1,16,896]{2,1,0:T(8,128)(2,1)S(1)}, bf16[1,16,896]{2,1,0:T(8,128)(2,1)S(1)}, u32[]{:S(2)}, u32[]{:S(2)}) collective-permute-start(bf16[1,16,896]{2,1,0:T(8,128)(2,1)S(1)} %shard_map.60), channel_id=1, source_target_pairs={{0,4},{16,20},{32,36},{48,52},{64,68},{80,84},{96,100},{112,116},{... | collective-permute-start | bytes 86024 | tf_op jit(solution)/shard_map/ppermute | solution.py:179
  24.9 1.9 %collective-permute-start.1 = (bf16[1,16,896]{2,1,0:T(8,128)(2,1)S(1)}, bf16[1,16,896]{2,1,0:T(8,128)(2,1)S(1)}, u32[]{:S(2)}, u32[]{:S(2)}) collective-permute-start(bf16[1,16,896]{2,1,0:T(8,128)(2,1)S(1)} %shard_map.60), channel_id=1, source_target_pairs={{0,68},{16,84},{32,100},{48,116},{64,0},{80,16},{96,32},{112,48},{... | collective-permute-start | bytes 86024 | tf_op jit(solution)/shard_map/ppermute | solution.py:179
  26.8 7.8 %collective-permute-start = (bf16[1,16,896]{2,1,0:T(8,128)(2,1)S(1)}, bf16[1,16,896]{2,1,0:T(8,128)(2,1)S(1)}, u32[]{:S(2)}, u32[]{:S(2)}) collective-permute-start(bf16[1,16,896]{2,1,0:T(8,128)(2,1)S(1)} %shard_map.60), channel_id=1, source_target_pairs={{0,64},{16,80},{32,96},{48,112},{64,4},{80,20},{96,36},{112,52},{4... | collective-permute-start | bytes 86024 | tf_op jit(solution)/shard_map/ppermute | solution.py:179
  34.7 0.0 collective-permute-done.2
  34.7 0.8 collective-permute-done.1
  35.5 1.7 %collective-permute-done = bf16[1,16,896]{2,1,0:T(8,128)(2,1)S(1)} collective-permute-done((bf16[1,16,896]{2,1,0:T(8,128)(2,1)S(1)}, bf16[1,16,896]{2,1,0:T(8,128)(2,1)S(1)}, u32[]{:S(2)}, u32[]{:S(2)}) %collective-permute-start) | collective-permute-done | bytes 28704 | tf_op jit(solution)/shard_map/ppermute | solution.py:179
  37.3 4.1 %collective-permute-start.5 = (bf16[4,16,896]{2,1,0:T(8,128)(2,1)S(1)}, bf16[4,16,896]{2,1,0:T(8,128)(2,1)S(1)}, u32[]{:S(2)}, u32[]{:S(2)}) collective-permute-start(bf16[4,16,896]{2,1,0:T(8,128)(2,1)S(1)} %pad_maximum_fusion.1.refs_0_), channel_id=1, source_target_pairs={{0,32},{16,116},{32,64},{48,16},{64,96},{80,48},{96,4},{112,80},{4... | collective-permute-start | bytes 344072 | tf_op jit(solution)/shard_map/ppermute | solution.py:179
  41.4 2.3 %collective-permute-start.4 = (bf16[4,16,896]{2,1,0:T(8,128)(2,1)S(1)}, bf16[4,16,896]{2,1,0:T(8,128)(2,1)S(1)}, u32[]{:S(2)}, u32[]{:S(2)}) collective-permute-start(bf16[4,16,896]{2,1,0:T(8,128)(2,1)S(1)} %pad_maximum_fusion.1.refs_0_), channel_id=1, source_target_pairs={{0,116},{16,0},{32,16},{48,32},{64,48},{80,64},{96,80},{112,96},{4... | collective-permute-start | bytes 344072 | tf_op jit(solution)/shard_map/ppermute | solution.py:179
  43.7 4.9 %collective-permute-start.3 = (bf16[4,16,896]{2,1,0:T(8,128)(2,1)S(1)}, bf16[4,16,896]{2,1,0:T(8,128)(2,1)S(1)}, u32[]{:S(2)}, u32[]{:S(2)}) collective-permute-start(bf16[4,16,896]{2,1,0:T(8,128)(2,1)S(1)} %pad_maximum_fusion.1.refs_0_), channel_id=1, source_target_pairs={{0,16},{16,32},{32,48},{48,64},{64,80},{80,96},{96,112},{112,4},{4... | collective-permute-start | bytes 344072 | tf_op jit(solution)/shard_map/ppermute | solution.py:179
  50.0 0.1 pad_add_fusion.place_ref
  50.1 0.0 collective-permute-done.5.refs_3_
  50.1 0.0 collective-permute-done.4.refs_2_
  50.1 1.0 collective-permute-done.3.refs_1_
  51.0 0.0 all-to-all-done.images_ref
  51.0 3.7 %shard_map.61 = (bf16[16,16,896]{2,1,0:T(8,128)(2,1)S(1)}, f32[16,16,896]{2,1,0:T(8,128)S(1)}, bf16[16,16,896]{2,1,0:T(8,128)(2,1)}) custom-call(f32[1]{0:T(128)S(6)} %copy.6.temp_ref, f32[1]{0:T(128)S(6)} %copy.7.bias_ref, s32[4]{0:T(128)S(1)} %pad_add_fusion.place_ref, bf16[32,16,896]{2,1,0:T(8,128)(2,1)S(1)} %all-to-all-done.images_ref, ...), custom_call_target="tpu_custom_call" | custom-call | flops 900000000 | bytes 4000000 | tf_op jit(solution)/shard_map/pallas_call | solution.py:126
  54.7 1.9 %collective-permute-start.6 = (bf16[16,16,896]{2,1,0:T(8,128)(2,1)S(1)}, bf16[16,16,896]{2,1,0:T(8,128)(2,1)S(1)}, u32[]{:S(2)}, u32[]{:S(2)}) collective-permute-start(bf16[16,16,896]{2,1,0:T(8,128)(2,1)S(1)} %get-tuple-element.6), channel_id=1, source_target_pairs={{0,8},{8,0},{1,9},{9,1},{2,10},{10,2},{3,11},{11,3},{4,12},{12,4},... | collective-permute-start | bytes 1376264 | tf_op jit(solution)/shard_map/ppermute | solution.py:184
  56.7 11.8 %all-to-all-start.1 = ((bf16[16,16,896]{2,1,0:T(8,128)(2,1)}), bf16[16,16,896]{2,1,0:T(8,128)(2,1)S(1)}, u32[]{:S(2)}, u32[]{:S(2)}) async-start(bf16[16,16,896]{2,1,0:T(8,128)(2,1)} %get-tuple-element.7), calls=%async_computation.1 | async-start | bytes 917504 | tf_op jit(solution)/shard_map/all_to_all | solution.py:198
  68.5 0.0 collective-permute-done.6
  68.5 0.1 fusion
  68.6 3.6 %collective-permute-start.7 = (bf16[4,16,896]{2,1,0:T(8,128)(2,1)S(1)}, bf16[4,16,896]{2,1,0:T(8,128)(2,1)S(1)}, u32[]{:S(2)}, u32[]{:S(2)}) collective-permute-start(bf16[4,16,896]{2,1,0:T(8,128)(2,1)S(1)} %get-tuple-element.10), channel_id=1, source_target_pairs={{0,1},{1,2},{2,3},{3,0},{4,5},{5,6},{6,7},{7,4},{8,9},{9,10},{10,1... | collective-permute-start | bytes 344072 | tf_op jit(solution)/shard_map/ppermute | solution.py:184
  72.2 4.6 %collective-permute-start.9 = (bf16[4,16,896]{2,1,0:T(8,128)(2,1)S(1)}, bf16[4,16,896]{2,1,0:T(8,128)(2,1)S(1)}, u32[]{:S(2)}, u32[]{:S(2)}) collective-permute-start(bf16[4,16,896]{2,1,0:T(8,128)(2,1)S(1)} %get-tuple-element.11), channel_id=1, source_target_pairs={{0,2},{1,3},{2,0},{3,1},{4,6},{5,7},{6,4},{7,5},{8,10},{9,11},{10,... | collective-permute-start | bytes 344072 | tf_op jit(solution)/shard_map/ppermute | solution.py:184
  76.8 3.4 %collective-permute-start.8 = (bf16[4,16,896]{2,1,0:T(8,128)(2,1)S(1)}, bf16[4,16,896]{2,1,0:T(8,128)(2,1)S(1)}, u32[]{:S(2)}, u32[]{:S(2)}) collective-permute-start(bf16[4,16,896]{2,1,0:T(8,128)(2,1)S(1)} %get-tuple-element.12), channel_id=1, source_target_pairs={{0,3},{1,0},{2,1},{3,2},{4,7},{5,4},{6,5},{7,6},{8,11},{9,8},{10,9... | collective-permute-start | bytes 344072 | tf_op jit(solution)/shard_map/ppermute | solution.py:184
  80.2 0.0 collective-permute-done.7
  80.2 0.2 collective-permute-done.9
  80.4 3.1 %collective-permute-done.8 = bf16[4,16,896]{2,1,0:T(8,128)(2,1)S(1)} collective-permute-done((bf16[4,16,896]{2,1,0:T(8,128)(2,1)S(1)}, bf16[4,16,896]{2,1,0:T(8,128)(2,1)S(1)}, u32[]{:S(2)}, u32[]{:S(2)}) %collective-permute-start.8) | collective-permute-done | bytes 114720 | tf_op jit(solution)/shard_map/ppermute | solution.py:184
  83.6 4.9 %collective-permute-start.12 = (f32[16,896]{1,0:T(8,128)S(1)}, f32[16,896]{1,0:T(8,128)S(1)}, u32[]{:S(2)}, u32[]{:S(2)}) collective-permute-start(f32[16,896]{1,0:T(8,128)S(1)} %get-tuple-element.14), channel_id=1, source_target_pairs={{0,256},{128,384},{256,0},{384,128},{1,257},{129,385},{257,1},{385... | collective-permute-start | bytes 172040 | tf_op jit(solution)/shard_map/ppermute | solution.py:184
  88.5 3.1 %collective-permute-start.11 = (f32[16,896]{1,0:T(8,128)S(1)}, f32[16,896]{1,0:T(8,128)S(1)}, u32[]{:S(2)}, u32[]{:S(2)}) collective-permute-start(f32[16,896]{1,0:T(8,128)S(1)} %get-tuple-element.15), channel_id=1, source_target_pairs={{0,384},{128,0},{256,128},{384,256},{1,385},{129,1},{257,129},{385... | collective-permute-start | bytes 172040 | tf_op jit(solution)/shard_map/ppermute | solution.py:184
  91.5 2.8 %collective-permute-start.10 = (f32[16,896]{1,0:T(8,128)S(1)}, f32[16,896]{1,0:T(8,128)S(1)}, u32[]{:S(2)}, u32[]{:S(2)}) collective-permute-start(f32[16,896]{1,0:T(8,128)S(1)} %get-tuple-element.16), channel_id=1, source_target_pairs={{0,128},{128,256},{256,384},{384,0},{1,129},{129,257},{257,385},{3... | collective-permute-start | bytes 172040 | tf_op jit(solution)/shard_map/ppermute | solution.py:184
  94.3 0.0 collective-permute-done.12
  94.3 0.2 collective-permute-done.11
  94.5 4.3 %collective-permute-done.10 = f32[16,896]{1,0:T(8,128)S(1)} collective-permute-done((f32[16,896]{1,0:T(8,128)S(1)}, f32[16,896]{1,0:T(8,128)S(1)}, u32[]{:S(2)}, u32[]{:S(2)}) %collective-permute-start.10) | collective-permute-done | bytes 57376 | tf_op jit(solution)/shard_map/ppermute | solution.py:184
  98.8 0.0 copy-start.2
  98.8 0.7 copy-done.2
  99.6 0.8 shard_map.62
  100.4 0.0 all-to-all-done.1.back_ref
  100.4 0.8 shard_map.63
  (5 shorter events, 0.1 us)
Async XLA Ops:
  0.6 0.8 copy-start.1
  2.5 7.5 %copy-start = (bf16[12,1152]{1,0:T(8,128)(2,1)S(1)}, bf16[12,1152]{1,0:T(8,128)(2,1)}, u32[]{:S(2)}) copy-start(bf16[12,1152]{1,0:T(8,128)(2,1)} %emb_ref.7) | copy-start | bytes 82948
  2.5 48.5 %all-to-all-start = ((bf16[32,16,896]{2,1,0:T(8,128)(2,1)}), bf16[32,16,896]{2,1,0:T(8,128)(2,1)S(1)}, u32[]{:S(2)}, u32[]{:S(2)}) async-start(bf16[32,16,896]{2,1,0:T(8,128)(2,1)} %shard_map.59), calls=%async_computation | async-start | bytes 1835008 | tf_op jit(solution)/shard_map/all_to_all | solution.py:191
  10.1 24.6 %collective-permute-start.2 = (bf16[1,16,896]{2,1,0:T(8,128)(2,1)S(1)}, bf16[1,16,896]{2,1,0:T(8,128)(2,1)S(1)}, u32[]{:S(2)}, u32[]{:S(2)}) collective-permute-start(bf16[1,16,896]{2,1,0:T(8,128)(2,1)S(1)} %shard_map.60), channel_id=1, source_target_pairs={{0,4},{16,20},{32,36},{48,52},{64,68},{80,84},{96,100},{112,116},{... | collective-permute-start | bytes 86024 | tf_op jit(solution)/shard_map/ppermute | solution.py:179
  24.9 10.6 %collective-permute-start.1 = (bf16[1,16,896]{2,1,0:T(8,128)(2,1)S(1)}, bf16[1,16,896]{2,1,0:T(8,128)(2,1)S(1)}, u32[]{:S(2)}, u32[]{:S(2)}) collective-permute-start(bf16[1,16,896]{2,1,0:T(8,128)(2,1)S(1)} %shard_map.60), channel_id=1, source_target_pairs={{0,68},{16,84},{32,100},{48,116},{64,0},{80,16},{96,32},{112,48},{... | collective-permute-start | bytes 86024 | tf_op jit(solution)/shard_map/ppermute | solution.py:179
  26.8 10.4 %collective-permute-start = (bf16[1,16,896]{2,1,0:T(8,128)(2,1)S(1)}, bf16[1,16,896]{2,1,0:T(8,128)(2,1)S(1)}, u32[]{:S(2)}, u32[]{:S(2)}) collective-permute-start(bf16[1,16,896]{2,1,0:T(8,128)(2,1)S(1)} %shard_map.60), channel_id=1, source_target_pairs={{0,64},{16,80},{32,96},{48,112},{64,4},{80,20},{96,36},{112,52},{4... | collective-permute-start | bytes 86024 | tf_op jit(solution)/shard_map/ppermute | solution.py:179
  37.3 12.8 %collective-permute-start.5 = (bf16[4,16,896]{2,1,0:T(8,128)(2,1)S(1)}, bf16[4,16,896]{2,1,0:T(8,128)(2,1)S(1)}, u32[]{:S(2)}, u32[]{:S(2)}) collective-permute-start(bf16[4,16,896]{2,1,0:T(8,128)(2,1)S(1)} %pad_maximum_fusion.1.refs_0_), channel_id=1, source_target_pairs={{0,32},{16,116},{32,64},{48,16},{64,96},{80,48},{96,4},{112,80},{4... | collective-permute-start | bytes 344072 | tf_op jit(solution)/shard_map/ppermute | solution.py:179
  41.4 8.7 %collective-permute-start.4 = (bf16[4,16,896]{2,1,0:T(8,128)(2,1)S(1)}, bf16[4,16,896]{2,1,0:T(8,128)(2,1)S(1)}, u32[]{:S(2)}, u32[]{:S(2)}) collective-permute-start(bf16[4,16,896]{2,1,0:T(8,128)(2,1)S(1)} %pad_maximum_fusion.1.refs_0_), channel_id=1, source_target_pairs={{0,116},{16,0},{32,16},{48,32},{64,48},{80,64},{96,80},{112,96},{4... | collective-permute-start | bytes 344072 | tf_op jit(solution)/shard_map/ppermute | solution.py:179
  43.7 7.3 %collective-permute-start.3 = (bf16[4,16,896]{2,1,0:T(8,128)(2,1)S(1)}, bf16[4,16,896]{2,1,0:T(8,128)(2,1)S(1)}, u32[]{:S(2)}, u32[]{:S(2)}) collective-permute-start(bf16[4,16,896]{2,1,0:T(8,128)(2,1)S(1)} %pad_maximum_fusion.1.refs_0_), channel_id=1, source_target_pairs={{0,16},{16,32},{32,48},{48,64},{64,80},{80,96},{96,112},{112,4},{4... | collective-permute-start | bytes 344072 | tf_op jit(solution)/shard_map/ppermute | solution.py:179
  54.7 13.7 %collective-permute-start.6 = (bf16[16,16,896]{2,1,0:T(8,128)(2,1)S(1)}, bf16[16,16,896]{2,1,0:T(8,128)(2,1)S(1)}, u32[]{:S(2)}, u32[]{:S(2)}) collective-permute-start(bf16[16,16,896]{2,1,0:T(8,128)(2,1)S(1)} %get-tuple-element.6), channel_id=1, source_target_pairs={{0,8},{8,0},{1,9},{9,1},{2,10},{10,2},{3,11},{11,3},{4,12},{12,4},... | collective-permute-start | bytes 1376264 | tf_op jit(solution)/shard_map/ppermute | solution.py:184
  56.7 43.8 %all-to-all-start.1 = ((bf16[16,16,896]{2,1,0:T(8,128)(2,1)}), bf16[16,16,896]{2,1,0:T(8,128)(2,1)S(1)}, u32[]{:S(2)}, u32[]{:S(2)}) async-start(bf16[16,16,896]{2,1,0:T(8,128)(2,1)} %get-tuple-element.7), calls=%async_computation.1 | async-start | bytes 917504 | tf_op jit(solution)/shard_map/all_to_all | solution.py:198
  68.6 11.5 %collective-permute-start.7 = (bf16[4,16,896]{2,1,0:T(8,128)(2,1)S(1)}, bf16[4,16,896]{2,1,0:T(8,128)(2,1)S(1)}, u32[]{:S(2)}, u32[]{:S(2)}) collective-permute-start(bf16[4,16,896]{2,1,0:T(8,128)(2,1)S(1)} %get-tuple-element.10), channel_id=1, source_target_pairs={{0,1},{1,2},{2,3},{3,0},{4,5},{5,6},{6,7},{7,4},{8,9},{9,10},{10,1... | collective-permute-start | bytes 344072 | tf_op jit(solution)/shard_map/ppermute | solution.py:184
  72.2 8.2 %collective-permute-start.9 = (bf16[4,16,896]{2,1,0:T(8,128)(2,1)S(1)}, bf16[4,16,896]{2,1,0:T(8,128)(2,1)S(1)}, u32[]{:S(2)}, u32[]{:S(2)}) collective-permute-start(bf16[4,16,896]{2,1,0:T(8,128)(2,1)S(1)} %get-tuple-element.11), channel_id=1, source_target_pairs={{0,2},{1,3},{2,0},{3,1},{4,6},{5,7},{6,4},{7,5},{8,10},{9,11},{10,... | collective-permute-start | bytes 344072 | tf_op jit(solution)/shard_map/ppermute | solution.py:184
  76.8 6.7 %collective-permute-start.8 = (bf16[4,16,896]{2,1,0:T(8,128)(2,1)S(1)}, bf16[4,16,896]{2,1,0:T(8,128)(2,1)S(1)}, u32[]{:S(2)}, u32[]{:S(2)}) collective-permute-start(bf16[4,16,896]{2,1,0:T(8,128)(2,1)S(1)} %get-tuple-element.12), channel_id=1, source_target_pairs={{0,3},{1,0},{2,1},{3,2},{4,7},{5,4},{6,5},{7,6},{8,11},{9,8},{10,9... | collective-permute-start | bytes 344072 | tf_op jit(solution)/shard_map/ppermute | solution.py:184
  83.6 10.8 %collective-permute-start.12 = (f32[16,896]{1,0:T(8,128)S(1)}, f32[16,896]{1,0:T(8,128)S(1)}, u32[]{:S(2)}, u32[]{:S(2)}) collective-permute-start(f32[16,896]{1,0:T(8,128)S(1)} %get-tuple-element.14), channel_id=1, source_target_pairs={{0,256},{128,384},{256,0},{384,128},{1,257},{129,385},{257,1},{385... | collective-permute-start | bytes 172040 | tf_op jit(solution)/shard_map/ppermute | solution.py:184
  88.5 6.1 %collective-permute-start.11 = (f32[16,896]{1,0:T(8,128)S(1)}, f32[16,896]{1,0:T(8,128)S(1)}, u32[]{:S(2)}, u32[]{:S(2)}) collective-permute-start(f32[16,896]{1,0:T(8,128)S(1)} %get-tuple-element.15), channel_id=1, source_target_pairs={{0,384},{128,0},{256,128},{384,256},{1,385},{129,1},{257,129},{385... | collective-permute-start | bytes 172040 | tf_op jit(solution)/shard_map/ppermute | solution.py:184
  91.5 7.3 %collective-permute-start.10 = (f32[16,896]{1,0:T(8,128)S(1)}, f32[16,896]{1,0:T(8,128)S(1)}, u32[]{:S(2)}, u32[]{:S(2)}) collective-permute-start(f32[16,896]{1,0:T(8,128)S(1)} %get-tuple-element.16), channel_id=1, source_target_pairs={{0,128},{128,256},{256,384},{384,0},{1,129},{129,257},{257,385},{3... | collective-permute-start | bytes 172040 | tf_op jit(solution)/shard_map/ppermute | solution.py:184
  98.8 0.8 copy-start.2
where the time goes:
time: 102 us; the launch traced here: 101 us
  starting transfers between devices  79.4 us (78%)
  waiting for transfers between devices  11.3 us (11%)
  Pallas kernels  6.59 us (6%)
  between operations  2.13 us (2%)
  local copies, waits for them, and re-layouts  1.56 us (2%)
    ppermute x6, starting transfers between devices, along_z(): return lax.ppermute(value, LINE, pairs)  36 us
    ppermute x7, starting transfers between devices, around(): return lax.ppermute(value, axis, [(i, (i + by) % n) for i in range(n)])  24.2 us
    all_to_all x1, starting transfers between devices, on_device(): text_back = lax.all_to_all(text_part, LINE, 0, 0)  11.8 us
    ppermute x7, waiting for transfers between devices, around(): return lax.ppermute(value, axis, [(i, (i + by) % n) for i in range(n)])  7.79 us
    all_to_all x1, starting transfers between devices, on_device(): lax.all_to_all(spread(image_embeds, lax.axis_size(PLANE)), PLANE, 0, 0)  7.45 us
    pallas_call x1, Pallas kernels, pair_terms(): pl.pallas_call(pair_kernel, in_specs=[pl.BlockSpec(memory_space=pltpu.SME...  3.73 us
    ppermute x6, waiting for transfers between devices, along_z(): return lax.ppermute(value, LINE, pairs)  3.5 us
  transfers between devices with their start and end apart: 15, of which 7 were waited for; matrix products, arithmetic and copies ran while one was open for 0% of the time, Pallas kernels for 1%

commit v1 on v0

v1 whole, which is shorter than its diff:
```python
import jax
import jax.numpy as jnp
from jax import lax
from jax.experimental import pallas as pl
from jax.experimental.pallas import tpu as pltpu
from jax.sharding import Mesh, PartitionSpec as P

EPS = 1e-06
AXES = ("x", "zm", "zn", "core", "zh", "y")
SIZES = (4, 2, 4, 2, 2, 4)
PLANE = ("x", "core", "y")
LINE = ("zm", "zn", "zh")
FAR = (0, 4, 12, 8)
VMEM = 48 * 1024 * 1024

ROWS = 12
WIDTH = 1152
TALL = 16
MAIN = 896
REST = WIDTH - MAIN
STEP = TALL - ROWS
PIECES = [
    (
        slice(m * STEP, (m + 1) * STEP),
        slice(g * 128, (g + 1) * 128),
        slice((3 * g + m) * 128, (3 * g + m + 1) * 128),
    )
    for g in range(REST // 128)
    for m in range(ROWS // STEP)
]


def spread_kernel(emb_ref, out_ref, unit_ref, inverse_ref, block):
    wide = emb_ref[...].astype(jnp.float32)
    inverse = lax.rsqrt(jnp.sum(wide * wide, axis=1, keepdims=True) + EPS)
    unit_ref[...] = wide * inverse
    inverse_ref[...] = inverse
    block[:ROWS, :] = unit_ref[:, :MAIN]
    block[ROWS:, :] = jnp.zeros((STEP, MAIN), jnp.float32)
    for rows, cols, place in PIECES:
        block[ROWS:, place] = unit_ref[rows, MAIN + cols.start : MAIN + cols.stop]
    out_ref[...] = jnp.broadcast_to(block[...].astype(jnp.bfloat16)[None], out_ref.shape)


def spread(emb, peers):
    return pl.pallas_call(
        spread_kernel,
        out_shape=[
            jax.ShapeDtypeStruct((peers, TALL, MAIN), jnp.bfloat16),
            jax.ShapeDtypeStruct(emb.shape, jnp.float32),
            jax.ShapeDtypeStruct((ROWS, 1), jnp.float32),
        ],
        scratch_shapes=[pltpu.VMEM((TALL, MAIN), jnp.float32)],
        compiler_params=pltpu.CompilerParams(vmem_limit_bytes=VMEM),
        cost_estimate=pl.CostEstimate(flops=100_000, bytes_accessed=1_000_000, transcendentals=0),
    )(emb)


def packed(main, rest, n):
    for rows, cols, place in PIECES:
        main[:n, ROWS:, place] = rest[:n, rows, cols]
    return main[:n]


def pair_kernel(temp_ref, bias_ref, place_ref, images_ref, *refs):
    text_refs = refs[:4]
    core_out, image_out, text_out = refs[4:7]
    texts, image_rest, coeff_ref, rest, main = refs[7:]
    n_images, far = images_ref.shape[0], text_refs[0].shape[0]
    rest[:, ROWS:, :] = jnp.zeros((n_images, STEP, REST), jnp.float32)

    def gather_rest(ref):
        n = ref.shape[0]
        for rows, cols, place in PIECES:
            rest[:n, rows, cols] = ref[:, ROWS:, place].astype(jnp.float32)
        return rest[:n].reshape(n * TALL, REST).astype(jnp.bfloat16)

    for i, ref in enumerate(text_refs):
        span = pl.ds(i * far * TALL, far * TALL)
        texts[span, :MAIN] = ref[...].reshape(far * TALL, MAIN)
        texts[span, MAIN:] = gather_rest(ref)
    image_rest[...] = gather_rest(images_ref)
    image_main = images_ref[...].reshape(n_images * TALL, MAIN)

    def dot(a, b, dims):
        return lax.dot_general(
            a, b, ((dims[:1], dims[1:]), ((), ())), preferred_element_type=jnp.float32
        )

    scale = jnp.exp(jnp.full((1, 1), temp_ref[0], jnp.float32))
    logits = dot(image_main, texts[:, :MAIN], (1, 1)) + dot(image_rest[...], texts[:, MAIN:], (1, 1))
    logits = scale * logits + bias_ref[0]
    x, core, y = place_ref[0] // 8, place_ref[0] // 4 % 2, place_ref[0] % 4
    z = place_ref[1]
    row = lax.broadcasted_iota(jnp.int32, logits.shape, 0)
    col = lax.broadcasted_iota(jnp.int32, logits.shape, 1)
    real = (row % TALL < ROWS) & (col % TALL < ROWS)
    same = (row == col + place_ref[0] * TALL) & (col < TALL)
    sig = jax.nn.sigmoid(jnp.where(same, -logits, logits))
    coeff_ref[...] = jnp.where(real, jnp.where(same, -sig, sig) * scale, 0.0).astype(jnp.bfloat16)
    coeff = coeff_ref[...]

    main[...] = dot(coeff, texts[:, :MAIN], (1, 0)).reshape(n_images, TALL, MAIN)
    rest[...] = dot(coeff, texts[:, MAIN:], (1, 0)).reshape(n_images, TALL, REST)
    packed(main, rest, n_images)
    for dy in range(4):
        for dx in range(4):
            spot = (x + dx) % 4 * 8 + (y + dy) % 4
            core_out[dy * 4 + dx] = main[spot + (1 - core) * 4].astype(jnp.bfloat16)
            image_out[dy * 4 + dx] = main[spot + core * 4]

    n = 4 * far
    main[:n] = dot(coeff, image_main, (0, 0)).reshape(n, TALL, MAIN)
    rest[:n] = dot(coeff, image_rest[...], (0, 0)).reshape(n, TALL, REST)
    packed(main, rest, n)
    for i, near in enumerate(near_moves(z)):
        for j, by in enumerate(FAR):
            source = (z - near - by + 32) % 16
            text_out[line_place(source)] = main[i * far + j].astype(jnp.bfloat16)


def pair_terms(log_temp, bias, place, images, texts):
    n_images, n_texts = images.shape[0], 4 * texts[0].shape[0]
    return pl.pallas_call(
        pair_kernel,
        in_specs=[pl.BlockSpec(memory_space=pltpu.SMEM)] * 3
        + [pl.BlockSpec(memory_space=pltpu.VMEM)] * 5,
        out_shape=[
            jax.ShapeDtypeStruct((n_images // 2, TALL, MAIN), jnp.bfloat16),
            jax.ShapeDtypeStruct((n_images // 2, TALL, MAIN), jnp.float32),
            jax.ShapeDtypeStruct((n_texts, TALL, MAIN), jnp.bfloat16),
        ],
        scratch_shapes=[
            pltpu.VMEM((n_texts * TALL, WIDTH), jnp.bfloat16),
            pltpu.VMEM((n_images * TALL, REST), jnp.bfloat16),
            pltpu.VMEM((n_images * TALL, n_texts * TALL), jnp.bfloat16),
            pltpu.VMEM((n_images, TALL, REST), jnp.float32),
            pltpu.VMEM((n_images, TALL, MAIN), jnp.float32),
        ],
        compiler_params=pltpu.CompilerParams(vmem_limit_bytes=VMEM),
        cost_estimate=pl.CostEstimate(
            flops=900_000_000, bytes_accessed=4_000_000, transcendentals=131_072
        ),
    )(log_temp, bias, place, images, *texts)


def finish_kernel(unit_ref, inverse_ref, *refs):
    back_refs, (out_ref, block) = refs[:-2], refs[-2:]
    total = sum(jnp.sum(ref[...].astype(jnp.float32), axis=0) for ref in back_refs)
    block[:, :MAIN] = total[:ROWS]
    for rows, cols, place in PIECES:
        block[rows, MAIN + cols.start : MAIN + cols.stop] = total[ROWS:, place]
    unit = unit_ref[...]
    direction = block[...]
    along = jnp.sum(unit * direction, axis=1, keepdims=True)
    out_ref[...] = (direction - unit * along) * inverse_ref[...]


def finish(unit, inverse, *back):
    return pl.pallas_call(
        finish_kernel,
        out_shape=jax.ShapeDtypeStruct(unit.shape, jnp.float32),
        scratch_shapes=[pltpu.VMEM((ROWS, WIDTH), jnp.float32)],
        compiler_params=pltpu.CompilerParams(vmem_limit_bytes=VMEM),
        cost_estimate=pl.CostEstimate(flops=500_000, bytes_accessed=1_000_000, transcendentals=0),
    )(unit, inverse, *back)


def line_place(z):
    return (z // 4 % 2) * 8 + (z % 4) * 2 + z // 8


def near_moves(z):
    return (0, 1, -1, 2 - 4 * (z % 2))


def along_z(value, move):
    pairs = [(line_place(z), line_place((z + move(z)) % 16)) for z in range(16)]
    return lax.ppermute(value, LINE, pairs)


def around(value, axis, by):
    n = lax.axis_size(axis)
    return lax.ppermute(value, axis, [(i, (i + by) % n) for i in range(n)])


def on_device(image_embeds, text_embeds, log_temp, bias):
    z = lax.axis_index("zh") * 8 + lax.axis_index("zm") * 4 + lax.axis_index("zn")
    place = jnp.stack([lax.axis_index(PLANE), z]).astype(jnp.int32)
    sent, img_unit, img_inv = spread(image_embeds, lax.axis_size(PLANE))
    own, txt_unit, txt_inv = spread(text_embeds, 1)

    images = lax.all_to_all(sent, PLANE, 0, 0)
    own = jnp.concatenate([own] + [along_z(own, lambda z, by=by: by) for by in FAR[1:]], axis=0)
    texts = [own] + [along_z(own, lambda z, i=i: near_moves(z)[i]) for i in (1, 2, 3)]

    core_part, part, text_part = pair_terms(log_temp, bias, place, images, texts)
    text_back = lax.all_to_all(text_part, LINE, 0, 0)
    part = part + around(core_part, "core", 1).astype(jnp.float32)
    part = part.reshape((4, 4) + part.shape[1:])
    part = part[0] + sum(
        around(part[by].astype(jnp.bfloat16), "y", by).astype(jnp.float32) for by in (1, 3, 2)
    )
    image_back = [part[:1]] + [around(part[by : by + 1], "x", by) for by in (1, 3, 2)]
    return (
        finish(img_unit, img_inv, *image_back),
        finish(txt_unit, txt_inv, text_back),
    )


def solution(mesh):
    fine = Mesh(mesh.devices.reshape(SIZES), AXES)
    split = P(AXES, None)
    return jax.shard_map(
        on_device,
        mesh=fine,
        in_specs=(split, split, P(), P()),
        out_specs=(split, split),
        check_vma=False,
    )
```

time: 102 us -> 103 us (level)
  waiting for transfers between devices: 11.3 us -> 13.1 us
    ppermute x7, waiting for transfers between devices: 7.79 us -> 9.57 us  [around(): return lax.ppermute(value, axis, [(i, (i + by) % n) for i in range(n)])]
where the time goes in v1:
time: 103 us; the launch traced here: 102 us
  starting transfers between devices  79.4 us (77%)
  waiting for transfers between devices  13.1 us (13%)
  Pallas kernels  6.48 us (6%)
  between operations  2.14 us (2%)
    ppermute x6, starting transfers between devices, along_z(): return lax.ppermute(value, LINE, pairs)  36 us
    ppermute x7, starting transfers between devices, around(): return lax.ppermute(value, axis, [(i, (i + by) % n) for i in range(n)])  24.2 us
    all_to_all x1, starting transfers between devices, on_device(): text_back = lax.all_to_all(text_part, LINE, 0, 0)  11.8 us
    ppermute x7, waiting for transfers between devices, around(): return lax.ppermute(value, axis, [(i, (i + by) % n) for i in range(n)])  9.57 us
    all_to_all x1, starting transfers between devices, on_device(): images = lax.all_to_all(sent, PLANE, 0, 0)  7.45 us
    pallas_call x1, Pallas kernels, pair_terms(): pl.pallas_call(pair_kernel, in_specs=[pl.BlockSpec(memory_space=pltpu.SME...  3.69 us
    ppermute x6, waiting for transfers between devices, along_z(): return lax.ppermute(value, LINE, pairs)  3.5 us
  transfers between devices with their start and end apart: 15, of which 7 were waited for; matrix products, arithmetic and copies ran while one was open for 0% of the time, Pallas kernels for 1%

profile of v1, /device:TPU:32, one launch (start us, length us, event | category | flops | bytes accessed | tf_op | source)
XLA Modules:
  0.0 102.1 jit_solution(3749058912897262950)
XLA Ops:
  0.6 0.0 copy-start
  0.6 0.8 copy-done
  1.4 1.1 %shard_map.59 = (bf16[32,16,896]{2,1,0:T(8,128)(2,1)}, f32[12,1152]{1,0:T(8,128)S(1)}, f32[12,1]{1,0:T(8,128)S(1)}) custom-call(bf16[12,1152]{1,0:T(8,128)(2,1)S(1)} %copy-done), custom_call_target="tpu_custom_call" | custom-call | flops 100000 | bytes 1000000 | tf_op jit(solution)/shard_map/pallas_call | solution.py:46
  2.5 0.0 copy-start.1
  2.5 7.5 %all-to-all-start = ((bf16[32,16,896]{2,1,0:T(8,128)(2,1)}), bf16[32,16,896]{2,1,0:T(8,128)(2,1)S(1)}, u32[]{:S(2)}, u32[]{:S(2)}) async-start(bf16[32,16,896]{2,1,0:T(8,128)(2,1)} %get-tuple-element.13), calls=%async_computation | async-start | bytes 1835008 | tf_op jit(solution)/shard_map/all_to_all | solution.py:193
  10.0 0.0 copy-done.1
  10.0 0.1 shard_map.60
  10.1 14.8 %collective-permute-start.2 = (bf16[1,16,896]{2,1,0:T(8,128)(2,1)S(1)}, bf16[1,16,896]{2,1,0:T(8,128)(2,1)S(1)}, u32[]{:S(2)}, u32[]{:S(2)}) collective-permute-start(bf16[1,16,896]{2,1,0:T(8,128)(2,1)S(1)} %get-tuple-element.14), channel_id=1, source_target_pairs={{0,4},{16,20},{32,36},{48,52},{64,68},{80,84},{96,100},{112,116},{... | collective-permute-start | bytes 86024 | tf_op jit(solution)/shard_map/ppermute | solution.py:179
  24.9 1.9 %collective-permute-start.1 = (bf16[1,16,896]{2,1,0:T(8,128)(2,1)S(1)}, bf16[1,16,896]{2,1,0:T(8,128)(2,1)S(1)}, u32[]{:S(2)}, u32[]{:S(2)}) collective-permute-start(bf16[1,16,896]{2,1,0:T(8,128)(2,1)S(1)} %get-tuple-element.14), channel_id=1, source_target_pairs={{0,68},{16,84},{32,100},{48,116},{64,0},{80,16},{96,32},{112,48},{... | collective-permute-start | bytes 86024 | tf_op jit(solution)/shard_map/ppermute | solution.py:179
  26.9 7.8 %collective-permute-start = (bf16[1,16,896]{2,1,0:T(8,128)(2,1)S(1)}, bf16[1,16,896]{2,1,0:T(8,128)(2,1)S(1)}, u32[]{:S(2)}, u32[]{:S(2)}) collective-permute-start(bf16[1,16,896]{2,1,0:T(8,128)(2,1)S(1)} %get-tuple-element.14), channel_id=1, source_target_pairs={{0,64},{16,80},{32,96},{48,112},{64,4},{80,20},{96,36},{112,52},{4... | collective-permute-start | bytes 86024 | tf_op jit(solution)/shard_map/ppermute | solution.py:179
  34.7 2.5 %collective-permute-done = bf16[1,16,896]{2,1,0:T(8,128)(2,1)S(1)} collective-permute-done((bf16[1,16,896]{2,1,0:T(8,128)(2,1)S(1)}, bf16[1,16,896]{2,1,0:T(8,128)(2,1)S(1)}, u32[]{:S(2)}, u32[]{:S(2)}) %collective-permute-start) | collective-permute-done | bytes 28704 | tf_op jit(solution)/shard_map/ppermute | solution.py:179
  37.3 0.0 collective-permute-done.1
  37.3 0.0 collective-permute-done.2
  37.3 4.1 %collective-permute-start.5 = (bf16[4,16,896]{2,1,0:T(8,128)(2,1)S(1)}, bf16[4,16,896]{2,1,0:T(8,128)(2,1)S(1)}, u32[]{:S(2)}, u32[]{:S(2)}) collective-permute-start(bf16[4,16,896]{2,1,0:T(8,128)(2,1)S(1)} %constant_dynamic-update-slice_fusion.refs_0_), channel_id=1, source_target_pairs={{0,32},{16,116},{32,64},{48,16},{64,96},{80,48},{96,4},{112,80},{4... | collective-permute-start | bytes 344072 | tf_op jit(solution)/shard_map/ppermute | solution.py:179
  41.4 2.3 %collective-permute-start.4 = (bf16[4,16,896]{2,1,0:T(8,128)(2,1)S(1)}, bf16[4,16,896]{2,1,0:T(8,128)(2,1)S(1)}, u32[]{:S(2)}, u32[]{:S(2)}) collective-permute-start(bf16[4,16,896]{2,1,0:T(8,128)(2,1)S(1)} %constant_dynamic-update-slice_fusion.refs_0_), channel_id=1, source_target_pairs={{0,116},{16,0},{32,16},{48,32},{64,48},{80,64},{96,80},{112,96},{4... | collective-permute-start | bytes 344072 | tf_op jit(solution)/shard_map/ppermute | solution.py:179
  43.8 4.9 %collective-permute-start.3 = (bf16[4,16,896]{2,1,0:T(8,128)(2,1)S(1)}, bf16[4,16,896]{2,1,0:T(8,128)(2,1)S(1)}, u32[]{:S(2)}, u32[]{:S(2)}) collective-permute-start(bf16[4,16,896]{2,1,0:T(8,128)(2,1)S(1)} %constant_dynamic-update-slice_fusion.refs_0_), channel_id=1, source_target_pairs={{0,16},{16,32},{32,48},{48,64},{64,80},{80,96},{96,112},{112,4},{4... | collective-permute-start | bytes 344072 | tf_op jit(solution)/shard_map/ppermute | solution.py:179
  50.0 0.1 pad_add_fusion.place_ref
  50.1 0.0 collective-permute-done.5.refs_3_
  50.1 0.0 collective-permute-done.4.refs_2_
  50.1 1.0 collective-permute-done.3.refs_1_
  51.0 0.0 all-to-all-done.images_ref
  51.1 3.7 %shard_map.61 = (bf16[16,16,896]{2,1,0:T(8,128)(2,1)S(1)}, f32[16,16,896]{2,1,0:T(8,128)S(1)}, bf16[16,16,896]{2,1,0:T(8,128)(2,1)}) custom-call(f32[1]{0:T(128)S(6)} %copy.9.temp_ref, f32[1]{0:T(128)S(6)} %copy.10.bias_ref, s32[2]{0:T(128)S(1)} %pad_add_fusion.place_ref, bf16[32,16,896]{2,1,0:T(8,128)(2,1)S(1)} %all-to-all-done.images_ref, ...), custom_call_target="tpu_custom_call" | custom-call | flops 900000000 | bytes 4000000 | tf_op jit(solution)/shard_map/pallas_call | solution.py:124
  54.7 11.8 %all-to-all-start.1 = ((bf16[16,16,896]{2,1,0:T(8,128)(2,1)}), bf16[16,16,896]{2,1,0:T(8,128)(2,1)S(1)}, u32[]{:S(2)}, u32[]{:S(2)}) async-start(bf16[16,16,896]{2,1,0:T(8,128)(2,1)} %get-tuple-element.19), calls=%async_computation.1 | async-start | bytes 917504 | tf_op jit(solution)/shard_map/all_to_all | solution.py:198
  66.5 1.9 %collective-permute-start.6 = (bf16[16,16,896]{2,1,0:T(8,128)(2,1)S(1)}, bf16[16,16,896]{2,1,0:T(8,128)(2,1)S(1)}, u32[]{:S(2)}, u32[]{:S(2)}) collective-permute-start(bf16[16,16,896]{2,1,0:T(8,128)(2,1)S(1)} %get-tuple-element.16), channel_id=1, source_target_pairs={{0,8},{8,0},{1,9},{9,1},{2,10},{10,2},{3,11},{11,3},{4,12},{12,4},... | collective-permute-start | bytes 1376264 | tf_op jit(solution)/shard_map/ppermute | solution.py:184
  68.4 1.8 %collective-permute-done.6 = bf16[16,16,896]{2,1,0:T(8,128)(2,1)S(1)} collective-permute-done((bf16[16,16,896]{2,1,0:T(8,128)(2,1)S(1)}, bf16[16,16,896]{2,1,0:T(8,128)(2,1)S(1)}, u32[]{:S(2)}, u32[]{:S(2)}) %collective-permute-start.6) | collective-permute-done | bytes 458784 | tf_op jit(solution)/shard_map/ppermute | solution.py:184
  70.2 0.1 fusion
  70.4 3.6 %collective-permute-start.7 = (bf16[4,16,896]{2,1,0:T(8,128)(2,1)S(1)}, bf16[4,16,896]{2,1,0:T(8,128)(2,1)S(1)}, u32[]{:S(2)}, u32[]{:S(2)}) collective-permute-start(bf16[4,16,896]{2,1,0:T(8,128)(2,1)S(1)} %get-tuple-element.22), channel_id=1, source_target_pairs={{0,1},{1,2},{2,3},{3,0},{4,5},{5,6},{6,7},{7,4},{8,9},{9,10},{10,1... | collective-permute-start | bytes 344072 | tf_op jit(solution)/shard_map/ppermute | solution.py:184
  74.0 4.6 %collective-permute-start.9 = (bf16[4,16,896]{2,1,0:T(8,128)(2,1)S(1)}, bf16[4,16,896]{2,1,0:T(8,128)(2,1)S(1)}, u32[]{:S(2)}, u32[]{:S(2)}) collective-permute-start(bf16[4,16,896]{2,1,0:T(8,128)(2,1)S(1)} %get-tuple-element.23), channel_id=1, source_target_pairs={{0,2},{1,3},{2,0},{3,1},{4,6},{5,7},{6,4},{7,5},{8,10},{9,11},{10,... | collective-permute-start | bytes 344072 | tf_op jit(solution)/shard_map/ppermute | solution.py:184
  78.5 3.4 %collective-permute-start.8 = (bf16[4,16,896]{2,1,0:T(8,128)(2,1)S(1)}, bf16[4,16,896]{2,1,0:T(8,128)(2,1)S(1)}, u32[]{:S(2)}, u32[]{:S(2)}) collective-permute-start(bf16[4,16,896]{2,1,0:T(8,128)(2,1)S(1)} %get-tuple-element.24), channel_id=1, source_target_pairs={{0,3},{1,0},{2,1},{3,2},{4,7},{5,4},{6,5},{7,6},{8,11},{9,8},{10,9... | collective-permute-start | bytes 344072 | tf_op jit(solution)/shard_map/ppermute | solution.py:184
  81.9 0.0 collective-permute-done.7
  81.9 0.3 collective-permute-done.9
  82.3 3.0 %collective-permute-done.8 = bf16[4,16,896]{2,1,0:T(8,128)(2,1)S(1)} collective-permute-done((bf16[4,16,896]{2,1,0:T(8,128)(2,1)S(1)}, bf16[4,16,896]{2,1,0:T(8,128)(2,1)S(1)}, u32[]{:S(2)}, u32[]{:S(2)}) %collective-permute-start.8) | collective-permute-done | bytes 114720 | tf_op jit(solution)/shard_map/ppermute | solution.py:184
  85.3 4.9 %collective-permute-start.12 = (f32[1,16,896]{2,1,0:T(8,128)S(1)}, f32[1,16,896]{2,1,0:T(8,128)S(1)}, u32[]{:S(2)}, u32[]{:S(2)}) collective-permute-start(f32[1,16,896]{2,1,0:T(8,128)S(1)} %get-tuple-element.25), channel_id=1, source_target_pairs={{0,256},{128,384},{256,0},{384,128},{1,257},{129,385},{257,1},{385... | collective-permute-start | bytes 172040 | tf_op jit(solution)/shard_map/ppermute | solution.py:184
  90.2 3.1 %collective-permute-start.11 = (f32[1,16,896]{2,1,0:T(8,128)S(1)}, f32[1,16,896]{2,1,0:T(8,128)S(1)}, u32[]{:S(2)}, u32[]{:S(2)}) collective-permute-start(f32[1,16,896]{2,1,0:T(8,128)S(1)} %get-tuple-element.26), channel_id=1, source_target_pairs={{0,384},{128,0},{256,128},{384,256},{1,385},{129,1},{257,129},{385... | collective-permute-start | bytes 172040 | tf_op jit(solution)/shard_map/ppermute | solution.py:184
  93.3 2.8 %collective-permute-start.10 = (f32[1,16,896]{2,1,0:T(8,128)S(1)}, f32[1,16,896]{2,1,0:T(8,128)S(1)}, u32[]{:S(2)}, u32[]{:S(2)}) collective-permute-start(f32[1,16,896]{2,1,0:T(8,128)S(1)} %get-tuple-element.27), channel_id=1, source_target_pairs={{0,128},{128,256},{256,384},{384,0},{1,129},{129,257},{257,385},{3... | collective-permute-start | bytes 172040 | tf_op jit(solution)/shard_map/ppermute | solution.py:184
  96.1 0.0 collective-permute-done.12.refs_3_
  96.1 0.2 collective-permute-done.11.refs_2_
  96.3 4.3 %collective-permute-done.10.refs_1_ = f32[1,16,896]{2,1,0:T(8,128)S(1)} collective-permute-done((f32[1,16,896]{2,1,0:T(8,128)S(1)}, f32[1,16,896]{2,1,0:T(8,128)S(1)}, u32[]{:S(2)}, u32[]{:S(2)}) %collective-permute-start.10) | collective-permute-done | bytes 57376 | tf_op jit(solution)/shard_map/ppermute | solution.py:184
  100.6 0.7 shard_map.62
  101.3 0.0 all-to-all-done.1.refs_0_
  101.3 0.8 shard_map.63
  (7 shorter events, 0.1 us)
Async XLA Ops:
  0.6 0.8 copy-start
  2.5 7.5 %copy-start.1 = (bf16[12,1152]{1,0:T(8,128)(2,1)S(1)}, bf16[12,1152]{1,0:T(8,128)(2,1)}, u32[]{:S(2)}) copy-start(bf16[12,1152]{1,0:T(8,128)(2,1)} %emb_ref.3) | copy-start | bytes 82948
  2.5 48.5 %all-to-all-start = ((bf16[32,16,896]{2,1,0:T(8,128)(2,1)}), bf16[32,16,896]{2,1,0:T(8,128)(2,1)S(1)}, u32[]{:S(2)}, u32[]{:S(2)}) async-start(bf16[32,16,896]{2,1,0:T(8,128)(2,1)} %get-tuple-element.13), calls=%async_computation | async-start | bytes 1835008 | tf_op jit(solution)/shard_map/all_to_all | solution.py:193
  10.1 27.2 %collective-permute-start.2 = (bf16[1,16,896]{2,1,0:T(8,128)(2,1)S(1)}, bf16[1,16,896]{2,1,0:T(8,128)(2,1)S(1)}, u32[]{:S(2)}, u32[]{:S(2)}) collective-permute-start(bf16[1,16,896]{2,1,0:T(8,128)(2,1)S(1)} %get-tuple-element.14), channel_id=1, source_target_pairs={{0,4},{16,20},{32,36},{48,52},{64,68},{80,84},{96,100},{112,116},{... | collective-permute-start | bytes 86024 | tf_op jit(solution)/shard_map/ppermute | solution.py:179
  24.9 12.3 %collective-permute-start.1 = (bf16[1,16,896]{2,1,0:T(8,128)(2,1)S(1)}, bf16[1,16,896]{2,1,0:T(8,128)(2,1)S(1)}, u32[]{:S(2)}, u32[]{:S(2)}) collective-permute-start(bf16[1,16,896]{2,1,0:T(8,128)(2,1)S(1)} %get-tuple-element.14), channel_id=1, source_target_pairs={{0,68},{16,84},{32,100},{48,116},{64,0},{80,16},{96,32},{112,48},{... | collective-permute-start | bytes 86024 | tf_op jit(solution)/shard_map/ppermute | solution.py:179
  26.9 10.4 %collective-permute-start = (bf16[1,16,896]{2,1,0:T(8,128)(2,1)S(1)}, bf16[1,16,896]{2,1,0:T(8,128)(2,1)S(1)}, u32[]{:S(2)}, u32[]{:S(2)}) collective-permute-start(bf16[1,16,896]{2,1,0:T(8,128)(2,1)S(1)} %get-tuple-element.14), channel_id=1, source_target_pairs={{0,64},{16,80},{32,96},{48,112},{64,4},{80,20},{96,36},{112,52},{4... | collective-permute-start | bytes 86024 | tf_op jit(solution)/shard_map/ppermute | solution.py:179
  37.3 12.8 %collective-permute-start.5 = (bf16[4,16,896]{2,1,0:T(8,128)(2,1)S(1)}, bf16[4,16,896]{2,1,0:T(8,128)(2,1)S(1)}, u32[]{:S(2)}, u32[]{:S(2)}) collective-permute-start(bf16[4,16,896]{2,1,0:T(8,128)(2,1)S(1)} %constant_dynamic-update-slice_fusion.refs_0_), channel_id=1, source_target_pairs={{0,32},{16,116},{32,64},{48,16},{64,96},{80,48},{96,4},{112,80},{4... | collective-permute-start | bytes 344072 | tf_op jit(solution)/shard_map/ppermute | solution.py:179
  41.4 8.7 %collective-permute-start.4 = (bf16[4,16,896]{2,1,0:T(8,128)(2,1)S(1)}, bf16[4,16,896]{2,1,0:T(8,128)(2,1)S(1)}, u32[]{:S(2)}, u32[]{:S(2)}) collective-permute-start(bf16[4,16,896]{2,1,0:T(8,128)(2,1)S(1)} %constant_dynamic-update-slice_fusion.refs_0_), channel_id=1, source_target_pairs={{0,116},{16,0},{32,16},{48,32},{64,48},{80,64},{96,80},{112,96},{4... | collective-permute-start | bytes 344072 | tf_op jit(solution)/shard_map/ppermute | solution.py:179
  43.8 7.3 %collective-permute-start.3 = (bf16[4,16,896]{2,1,0:T(8,128)(2,1)S(1)}, bf16[4,16,896]{2,1,0:T(8,128)(2,1)S(1)}, u32[]{:S(2)}, u32[]{:S(2)}) collective-permute-start(bf16[4,16,896]{2,1,0:T(8,128)(2,1)S(1)} %constant_dynamic-update-slice_fusion.refs_0_), channel_id=1, source_target_pairs={{0,16},{16,32},{32,48},{48,64},{64,80},{80,96},{96,112},{112,4},{4... | collective-permute-start | bytes 344072 | tf_op jit(solution)/shard_map/ppermute | solution.py:179
  54.7 46.6 %all-to-all-start.1 = ((bf16[16,16,896]{2,1,0:T(8,128)(2,1)}), bf16[16,16,896]{2,1,0:T(8,128)(2,1)S(1)}, u32[]{:S(2)}, u32[]{:S(2)}) async-start(bf16[16,16,896]{2,1,0:T(8,128)(2,1)} %get-tuple-element.19), calls=%async_computation.1 | async-start | bytes 917504 | tf_op jit(solution)/shard_map/all_to_all | solution.py:198
  66.5 3.7 %collective-permute-start.6 = (bf16[16,16,896]{2,1,0:T(8,128)(2,1)S(1)}, bf16[16,16,896]{2,1,0:T(8,128)(2,1)S(1)}, u32[]{:S(2)}, u32[]{:S(2)}) collective-permute-start(bf16[16,16,896]{2,1,0:T(8,128)(2,1)S(1)} %get-tuple-element.16), channel_id=1, source_target_pairs={{0,8},{8,0},{1,9},{9,1},{2,10},{10,2},{3,11},{11,3},{4,12},{12,4},... | collective-permute-start | bytes 1376264 | tf_op jit(solution)/shard_map/ppermute | solution.py:184
  70.4 11.6 %collective-permute-start.7 = (bf16[4,16,896]{2,1,0:T(8,128)(2,1)S(1)}, bf16[4,16,896]{2,1,0:T(8,128)(2,1)S(1)}, u32[]{:S(2)}, u32[]{:S(2)}) collective-permute-start(bf16[4,16,896]{2,1,0:T(8,128)(2,1)S(1)} %get-tuple-element.22), channel_id=1, source_target_pairs={{0,1},{1,2},{2,3},{3,0},{4,5},{5,6},{6,7},{7,4},{8,9},{9,10},{10,1... | collective-permute-start | bytes 344072 | tf_op jit(solution)/shard_map/ppermute | solution.py:184
  74.0 8.3 %collective-permute-start.9 = (bf16[4,16,896]{2,1,0:T(8,128)(2,1)S(1)}, bf16[4,16,896]{2,1,0:T(8,128)(2,1)S(1)}, u32[]{:S(2)}, u32[]{:S(2)}) collective-permute-start(bf16[4,16,896]{2,1,0:T(8,128)(2,1)S(1)} %get-tuple-element.23), channel_id=1, source_target_pairs={{0,2},{1,3},{2,0},{3,1},{4,6},{5,7},{6,4},{7,5},{8,10},{9,11},{10,... | collective-permute-start | bytes 344072 | tf_op jit(solution)/shard_map/ppermute | solution.py:184
  78.5 6.7 %collective-permute-start.8 = (bf16[4,16,896]{2,1,0:T(8,128)(2,1)S(1)}, bf16[4,16,896]{2,1,0:T(8,128)(2,1)S(1)}, u32[]{:S(2)}, u32[]{:S(2)}) collective-permute-start(bf16[4,16,896]{2,1,0:T(8,128)(2,1)S(1)} %get-tuple-element.24), channel_id=1, source_target_pairs={{0,3},{1,0},{2,1},{3,2},{4,7},{5,4},{6,5},{7,6},{8,11},{9,8},{10,9... | collective-permute-start | bytes 344072 | tf_op jit(solution)/shard_map/ppermute | solution.py:184
  85.3 10.8 %collective-permute-start.12 = (f32[1,16,896]{2,1,0:T(8,128)S(1)}, f32[1,16,896]{2,1,0:T(8,128)S(1)}, u32[]{:S(2)}, u32[]{:S(2)}) collective-permute-start(f32[1,16,896]{2,1,0:T(8,128)S(1)} %get-tuple-element.25), channel_id=1, source_target_pairs={{0,256},{128,384},{256,0},{384,128},{1,257},{129,385},{257,1},{385... | collective-permute-start | bytes 172040 | tf_op jit(solution)/shard_map/ppermute | solution.py:184
  90.2 6.1 %collective-permute-start.11 = (f32[1,16,896]{2,1,0:T(8,128)S(1)}, f32[1,16,896]{2,1,0:T(8,128)S(1)}, u32[]{:S(2)}, u32[]{:S(2)}) collective-permute-start(f32[1,16,896]{2,1,0:T(8,128)S(1)} %get-tuple-element.26), channel_id=1, source_target_pairs={{0,384},{128,0},{256,128},{384,256},{1,385},{129,1},{257,129},{385... | collective-permute-start | bytes 172040 | tf_op jit(solution)/shard_map/ppermute | solution.py:184
  93.3 7.3 %collective-permute-start.10 = (f32[1,16,896]{2,1,0:T(8,128)S(1)}, f32[1,16,896]{2,1,0:T(8,128)S(1)}, u32[]{:S(2)}, u32[]{:S(2)}) collective-permute-start(f32[1,16,896]{2,1,0:T(8,128)S(1)} %get-tuple-element.27), channel_id=1, source_target_pairs={{0,128},{128,256},{256,384},{384,0},{1,129},{129,257},{257,385},{3... | collective-permute-start | bytes 172040 | tf_op jit(solution)/shard_map/ppermute | solution.py:184

commit v2 on v1

--- a/solution.py
+++ b/solution.py
@@ -201,9 +201,9 @@
     part = part[0] + sum(
         around(part[by].astype(jnp.bfloat16), "y", by).astype(jnp.float32) for by in (1, 3, 2)
     )
-    image_back = [part[:1]] + [around(part[by : by + 1], "x", by) for by in (1, 3, 2)]
+    image_back = jnp.stack([part[0]] + [around(part[by], "x", by) for by in (1, 3, 2)], axis=0)
     return (
-        finish(img_unit, img_inv, *image_back),
+        finish(img_unit, img_inv, image_back),
         finish(txt_unit, txt_inv, text_back),
     )
 

time: 103 us -> 101 us (0.981)
  waiting for transfers between devices: 13.1 us -> 11.3 us
    ppermute x7, waiting for transfers between devices: 9.57 us -> 7.79 us  [around(): return lax.ppermute(value, axis, [(i, (i + by) % n) for i in range(n)])]
  transfers between devices with their start and end apart: 15 -> 15, of which waited for: 7 -> 6; matrix products, arithmetic and copies ran while one was open for 0% -> 0% of each run, Pallas kernels for 1% -> 1%
where the time goes in v2:
time: 101 us; the launch traced here: 100 us
  starting transfers between devices  79.4 us (79%)
  waiting for transfers between devices  11.3 us (11%)
  Pallas kernels  6.48 us (6%)
  between operations  2.15 us (2%)
    ppermute x6, starting transfers between devices, along_z(): return lax.ppermute(value, LINE, pairs)  36 us
    ppermute x7, starting transfers between devices, around(): return lax.ppermute(value, axis, [(i, (i + by) % n) for i in range(n)])  24.2 us
    all_to_all x1, starting transfers between devices, on_device(): text_back = lax.all_to_all(text_part, LINE, 0, 0)  11.8 us
    ppermute x7, waiting for transfers between devices, around(): return lax.ppermute(value, axis, [(i, (i + by) % n) for i in range(n)])  7.79 us
    all_to_all x1, starting transfers between devices, on_device(): images = lax.all_to_all(sent, PLANE, 0, 0)  7.45 us
    pallas_call x1, Pallas kernels, pair_terms(): pl.pallas_call(pair_kernel, in_specs=[pl.BlockSpec(memory_space=pltpu.SME...  3.69 us
    ppermute x6, waiting for transfers between devices, along_z(): return lax.ppermute(value, LINE, pairs)  3.5 us
  transfers between devices with their start and end apart: 15, of which 6 were waited for; matrix products, arithmetic and copies ran while one was open for 0% of the time, Pallas kernels for 1%

profile of v2, /device:TPU:32, one launch (start us, length us, event | category | flops | bytes accessed | tf_op | source)
XLA Modules:
  0.0 100.4 jit_solution(12947709707476901290)
XLA Ops:
  0.6 0.0 copy-start
  0.6 0.8 copy-done
  1.4 1.1 %shard_map.59 = (bf16[32,16,896]{2,1,0:T(8,128)(2,1)}, f32[12,1152]{1,0:T(8,128)S(1)}, f32[12,1]{1,0:T(8,128)S(1)}) custom-call(bf16[12,1152]{1,0:T(8,128)(2,1)S(1)} %copy-done), custom_call_target="tpu_custom_call" | custom-call | flops 100000 | bytes 1000000 | tf_op jit(solution)/shard_map/pallas_call | solution.py:46
  2.5 0.0 copy-start.1
  2.5 7.5 %all-to-all-start = ((bf16[32,16,896]{2,1,0:T(8,128)(2,1)}), bf16[32,16,896]{2,1,0:T(8,128)(2,1)S(1)}, u32[]{:S(2)}, u32[]{:S(2)}) async-start(bf16[32,16,896]{2,1,0:T(8,128)(2,1)} %get-tuple-element.13), calls=%async_computation | async-start | bytes 1835008 | tf_op jit(solution)/shard_map/all_to_all | solution.py:193
  10.0 0.0 copy-done.1
  10.0 0.1 shard_map.60
  10.1 14.8 %collective-permute-start.2 = (bf16[1,16,896]{2,1,0:T(8,128)(2,1)S(1)}, bf16[1,16,896]{2,1,0:T(8,128)(2,1)S(1)}, u32[]{:S(2)}, u32[]{:S(2)}) collective-permute-start(bf16[1,16,896]{2,1,0:T(8,128)(2,1)S(1)} %get-tuple-element.14), channel_id=1, source_target_pairs={{0,4},{16,20},{32,36},{48,52},{64,68},{80,84},{96,100},{112,116},{... | collective-permute-start | bytes 86024 | tf_op jit(solution)/shard_map/ppermute | solution.py:179
  24.9 1.9 %collective-permute-start.1 = (bf16[1,16,896]{2,1,0:T(8,128)(2,1)S(1)}, bf16[1,16,896]{2,1,0:T(8,128)(2,1)S(1)}, u32[]{:S(2)}, u32[]{:S(2)}) collective-permute-start(bf16[1,16,896]{2,1,0:T(8,128)(2,1)S(1)} %get-tuple-element.14), channel_id=1, source_target_pairs={{0,68},{16,84},{32,100},{48,116},{64,0},{80,16},{96,32},{112,48},{... | collective-permute-start | bytes 86024 | tf_op jit(solution)/shard_map/ppermute | solution.py:179
  26.9 7.8 %collective-permute-start = (bf16[1,16,896]{2,1,0:T(8,128)(2,1)S(1)}, bf16[1,16,896]{2,1,0:T(8,128)(2,1)S(1)}, u32[]{:S(2)}, u32[]{:S(2)}) collective-permute-start(bf16[1,16,896]{2,1,0:T(8,128)(2,1)S(1)} %get-tuple-element.14), channel_id=1, source_target_pairs={{0,64},{16,80},{32,96},{48,112},{64,4},{80,20},{96,36},{112,52},{4... | collective-permute-start | bytes 86024 | tf_op jit(solution)/shard_map/ppermute | solution.py:179
  34.7 2.5 %collective-permute-done = bf16[1,16,896]{2,1,0:T(8,128)(2,1)S(1)} collective-permute-done((bf16[1,16,896]{2,1,0:T(8,128)(2,1)S(1)}, bf16[1,16,896]{2,1,0:T(8,128)(2,1)S(1)}, u32[]{:S(2)}, u32[]{:S(2)}) %collective-permute-start) | collective-permute-done | bytes 28704 | tf_op jit(solution)/shard_map/ppermute | solution.py:179
  37.3 0.0 collective-permute-done.1
  37.3 0.0 collective-permute-done.2
  37.3 4.1 %collective-permute-start.5 = (bf16[4,16,896]{2,1,0:T(8,128)(2,1)S(1)}, bf16[4,16,896]{2,1,0:T(8,128)(2,1)S(1)}, u32[]{:S(2)}, u32[]{:S(2)}) collective-permute-start(bf16[4,16,896]{2,1,0:T(8,128)(2,1)S(1)} %constant_dynamic-update-slice_fusion.refs_0_), channel_id=1, source_target_pairs={{0,32},{16,116},{32,64},{48,16},{64,96},{80,48},{96,4},{112,80},{4... | collective-permute-start | bytes 344072 | tf_op jit(solution)/shard_map/ppermute | solution.py:179
  41.4 2.3 %collective-permute-start.4 = (bf16[4,16,896]{2,1,0:T(8,128)(2,1)S(1)}, bf16[4,16,896]{2,1,0:T(8,128)(2,1)S(1)}, u32[]{:S(2)}, u32[]{:S(2)}) collective-permute-start(bf16[4,16,896]{2,1,0:T(8,128)(2,1)S(1)} %constant_dynamic-update-slice_fusion.refs_0_), channel_id=1, source_target_pairs={{0,116},{16,0},{32,16},{48,32},{64,48},{80,64},{96,80},{112,96},{4... | collective-permute-start | bytes 344072 | tf_op jit(solution)/shard_map/ppermute | solution.py:179
  43.8 4.9 %collective-permute-start.3 = (bf16[4,16,896]{2,1,0:T(8,128)(2,1)S(1)}, bf16[4,16,896]{2,1,0:T(8,128)(2,1)S(1)}, u32[]{:S(2)}, u32[]{:S(2)}) collective-permute-start(bf16[4,16,896]{2,1,0:T(8,128)(2,1)S(1)} %constant_dynamic-update-slice_fusion.refs_0_), channel_id=1, source_target_pairs={{0,16},{16,32},{32,48},{48,64},{64,80},{80,96},{96,112},{112,4},{4... | collective-permute-start | bytes 344072 | tf_op jit(solution)/shard_map/ppermute | solution.py:179
  50.0 0.1 pad_add_fusion.place_ref
  50.1 0.0 collective-permute-done.5.refs_3_
  50.1 0.0 collective-permute-done.4.refs_2_
  50.1 1.0 collective-permute-done.3.refs_1_
  51.0 0.0 all-to-all-done.images_ref
  51.1 3.7 %shard_map.61 = (bf16[16,16,896]{2,1,0:T(8,128)(2,1)S(1)}, f32[16,16,896]{2,1,0:T(8,128)S(1)}, bf16[16,16,896]{2,1,0:T(8,128)(2,1)}) custom-call(f32[1]{0:T(128)S(6)} %copy.9.temp_ref, f32[1]{0:T(128)S(6)} %copy.10.bias_ref, s32[2]{0:T(128)S(1)} %pad_add_fusion.place_ref, bf16[32,16,896]{2,1,0:T(8,128)(2,1)S(1)} %all-to-all-done.images_ref, ...), custom_call_target="tpu_custom_call" | custom-call | flops 900000000 | bytes 4000000 | tf_op jit(solution)/shard_map/pallas_call | solution.py:124
  54.7 1.9 %collective-permute-start.6 = (bf16[16,16,896]{2,1,0:T(8,128)(2,1)S(1)}, bf16[16,16,896]{2,1,0:T(8,128)(2,1)S(1)}, u32[]{:S(2)}, u32[]{:S(2)}) collective-permute-start(bf16[16,16,896]{2,1,0:T(8,128)(2,1)S(1)} %get-tuple-element.16), channel_id=1, source_target_pairs={{0,8},{8,0},{1,9},{9,1},{2,10},{10,2},{3,11},{11,3},{4,12},{12,4},... | collective-permute-start | bytes 1376264 | tf_op jit(solution)/shard_map/ppermute | solution.py:184
  56.7 11.8 %all-to-all-start.1 = ((bf16[16,16,896]{2,1,0:T(8,128)(2,1)}), bf16[16,16,896]{2,1,0:T(8,128)(2,1)S(1)}, u32[]{:S(2)}, u32[]{:S(2)}) async-start(bf16[16,16,896]{2,1,0:T(8,128)(2,1)} %get-tuple-element.19), calls=%async_computation.1 | async-start | bytes 917504 | tf_op jit(solution)/shard_map/all_to_all | solution.py:198
  68.5 0.0 collective-permute-done.6
  68.5 0.1 fusion
  68.6 3.6 %collective-permute-start.7 = (bf16[4,16,896]{2,1,0:T(8,128)(2,1)S(1)}, bf16[4,16,896]{2,1,0:T(8,128)(2,1)S(1)}, u32[]{:S(2)}, u32[]{:S(2)}) collective-permute-start(bf16[4,16,896]{2,1,0:T(8,128)(2,1)S(1)} %get-tuple-element.22), channel_id=1, source_target_pairs={{0,1},{1,2},{2,3},{3,0},{4,5},{5,6},{6,7},{7,4},{8,9},{9,10},{10,1... | collective-permute-start | bytes 344072 | tf_op jit(solution)/shard_map/ppermute | solution.py:184
  72.2 4.6 %collective-permute-start.9 = (bf16[4,16,896]{2,1,0:T(8,128)(2,1)S(1)}, bf16[4,16,896]{2,1,0:T(8,128)(2,1)S(1)}, u32[]{:S(2)}, u32[]{:S(2)}) collective-permute-start(bf16[4,16,896]{2,1,0:T(8,128)(2,1)S(1)} %get-tuple-element.23), channel_id=1, source_target_pairs={{0,2},{1,3},{2,0},{3,1},{4,6},{5,7},{6,4},{7,5},{8,10},{9,11},{10,... | collective-permute-start | bytes 344072 | tf_op jit(solution)/shard_map/ppermute | solution.py:184
  76.8 3.4 %collective-permute-start.8 = (bf16[4,16,896]{2,1,0:T(8,128)(2,1)S(1)}, bf16[4,16,896]{2,1,0:T(8,128)(2,1)S(1)}, u32[]{:S(2)}, u32[]{:S(2)}) collective-permute-start(bf16[4,16,896]{2,1,0:T(8,128)(2,1)S(1)} %get-tuple-element.24), channel_id=1, source_target_pairs={{0,3},{1,0},{2,1},{3,2},{4,7},{5,4},{6,5},{7,6},{8,11},{9,8},{10,9... | collective-permute-start | bytes 344072 | tf_op jit(solution)/shard_map/ppermute | solution.py:184
  80.2 0.0 collective-permute-done.7
  80.2 0.2 collective-permute-done.9
  80.4 3.1 %collective-permute-done.8 = bf16[4,16,896]{2,1,0:T(8,128)(2,1)S(1)} collective-permute-done((bf16[4,16,896]{2,1,0:T(8,128)(2,1)S(1)}, bf16[4,16,896]{2,1,0:T(8,128)(2,1)S(1)}, u32[]{:S(2)}, u32[]{:S(2)}) %collective-permute-start.8) | collective-permute-done | bytes 114720 | tf_op jit(solution)/shard_map/ppermute | solution.py:184
  83.5 4.9 %collective-permute-start.12 = (f32[16,896]{1,0:T(8,128)S(1)}, f32[16,896]{1,0:T(8,128)S(1)}, u32[]{:S(2)}, u32[]{:S(2)}) collective-permute-start(f32[16,896]{1,0:T(8,128)S(1)} %get-tuple-element.26), channel_id=1, source_target_pairs={{0,256},{128,384},{256,0},{384,128},{1,257},{129,385},{257,1},{385... | collective-permute-start | bytes 172040 | tf_op jit(solution)/shard_map/ppermute | solution.py:184
  88.4 3.1 %collective-permute-start.11 = (f32[16,896]{1,0:T(8,128)S(1)}, f32[16,896]{1,0:T(8,128)S(1)}, u32[]{:S(2)}, u32[]{:S(2)}) collective-permute-start(f32[16,896]{1,0:T(8,128)S(1)} %get-tuple-element.27), channel_id=1, source_target_pairs={{0,384},{128,0},{256,128},{384,256},{1,385},{129,1},{257,129},{385... | collective-permute-start | bytes 172040 | tf_op jit(solution)/shard_map/ppermute | solution.py:184
  91.5 2.8 %collective-permute-start.10 = (f32[16,896]{1,0:T(8,128)S(1)}, f32[16,896]{1,0:T(8,128)S(1)}, u32[]{:S(2)}, u32[]{:S(2)}) collective-permute-start(f32[16,896]{1,0:T(8,128)S(1)} %get-tuple-element.28), channel_id=1, source_target_pairs={{0,128},{128,256},{256,384},{384,0},{1,129},{129,257},{257,385},{3... | collective-permute-start | bytes 172040 | tf_op jit(solution)/shard_map/ppermute | solution.py:184
  94.3 0.0 collective-permute-done.12
  94.3 0.2 collective-permute-done.11
  94.5 4.3 %collective-permute-done.10 = f32[16,896]{1,0:T(8,128)S(1)} collective-permute-done((f32[16,896]{1,0:T(8,128)S(1)}, f32[16,896]{1,0:T(8,128)S(1)}, u32[]{:S(2)}, u32[]{:S(2)}) %collective-permute-start.10) | collective-permute-done | bytes 57376 | tf_op jit(solution)/shard_map/ppermute | solution.py:184
  98.8 0.7 shard_map.62
  99.6 0.0 all-to-all-done.1.refs_0_
  99.6 0.8 shard_map.63
  (8 shorter events, 0.1 us)
Async XLA Ops:
  0.6 0.8 copy-start
  2.5 7.5 %copy-start.1 = (bf16[12,1152]{1,0:T(8,128)(2,1)S(1)}, bf16[12,1152]{1,0:T(8,128)(2,1)}, u32[]{:S(2)}) copy-start(bf16[12,1152]{1,0:T(8,128)(2,1)} %emb_ref.3) | copy-start | bytes 82948
  2.5 48.5 %all-to-all-start = ((bf16[32,16,896]{2,1,0:T(8,128)(2,1)}), bf16[32,16,896]{2,1,0:T(8,128)(2,1)S(1)}, u32[]{:S(2)}, u32[]{:S(2)}) async-start(bf16[32,16,896]{2,1,0:T(8,128)(2,1)} %get-tuple-element.13), calls=%async_computation | async-start | bytes 1835008 | tf_op jit(solution)/shard_map/all_to_all | solution.py:193
  10.1 27.2 %collective-permute-start.2 = (bf16[1,16,896]{2,1,0:T(8,128)(2,1)S(1)}, bf16[1,16,896]{2,1,0:T(8,128)(2,1)S(1)}, u32[]{:S(2)}, u32[]{:S(2)}) collective-permute-start(bf16[1,16,896]{2,1,0:T(8,128)(2,1)S(1)} %get-tuple-element.14), channel_id=1, source_target_pairs={{0,4},{16,20},{32,36},{48,52},{64,68},{80,84},{96,100},{112,116},{... | collective-permute-start | bytes 86024 | tf_op jit(solution)/shard_map/ppermute | solution.py:179
  24.9 12.3 %collective-permute-start.1 = (bf16[1,16,896]{2,1,0:T(8,128)(2,1)S(1)}, bf16[1,16,896]{2,1,0:T(8,128)(2,1)S(1)}, u32[]{:S(2)}, u32[]{:S(2)}) collective-permute-start(bf16[1,16,896]{2,1,0:T(8,128)(2,1)S(1)} %get-tuple-element.14), channel_id=1, source_target_pairs={{0,68},{16,84},{32,100},{48,116},{64,0},{80,16},{96,32},{112,48},{... | collective-permute-start | bytes 86024 | tf_op jit(solution)/shard_map/ppermute | solution.py:179
  26.9 10.4 %collective-permute-start = (bf16[1,16,896]{2,1,0:T(8,128)(2,1)S(1)}, bf16[1,16,896]{2,1,0:T(8,128)(2,1)S(1)}, u32[]{:S(2)}, u32[]{:S(2)}) collective-permute-start(bf16[1,16,896]{2,1,0:T(8,128)(2,1)S(1)} %get-tuple-element.14), channel_id=1, source_target_pairs={{0,64},{16,80},{32,96},{48,112},{64,4},{80,20},{96,36},{112,52},{4... | collective-permute-start | bytes 86024 | tf_op jit(solution)/shard_map/ppermute | solution.py:179
  37.3 12.8 %collective-permute-start.5 = (bf16[4,16,896]{2,1,0:T(8,128)(2,1)S(1)}, bf16[4,16,896]{2,1,0:T(8,128)(2,1)S(1)}, u32[]{:S(2)}, u32[]{:S(2)}) collective-permute-start(bf16[4,16,896]{2,1,0:T(8,128)(2,1)S(1)} %constant_dynamic-update-slice_fusion.refs_0_), channel_id=1, source_target_pairs={{0,32},{16,116},{32,64},{48,16},{64,96},{80,48},{96,4},{112,80},{4... | collective-permute-start | bytes 344072 | tf_op jit(solution)/shard_map/ppermute | solution.py:179
  41.4 8.7 %collective-permute-start.4 = (bf16[4,16,896]{2,1,0:T(8,128)(2,1)S(1)}, bf16[4,16,896]{2,1,0:T(8,128)(2,1)S(1)}, u32[]{:S(2)}, u32[]{:S(2)}) collective-permute-start(bf16[4,16,896]{2,1,0:T(8,128)(2,1)S(1)} %constant_dynamic-update-slice_fusion.refs_0_), channel_id=1, source_target_pairs={{0,116},{16,0},{32,16},{48,32},{64,48},{80,64},{96,80},{112,96},{4... | collective-permute-start | bytes 344072 | tf_op jit(solution)/shard_map/ppermute | solution.py:179
  43.8 7.3 %collective-permute-start.3 = (bf16[4,16,896]{2,1,0:T(8,128)(2,1)S(1)}, bf16[4,16,896]{2,1,0:T(8,128)(2,1)S(1)}, u32[]{:S(2)}, u32[]{:S(2)}) collective-permute-start(bf16[4,16,896]{2,1,0:T(8,128)(2,1)S(1)} %constant_dynamic-update-slice_fusion.refs_0_), channel_id=1, source_target_pairs={{0,16},{16,32},{32,48},{48,64},{64,80},{80,96},{96,112},{112,4},{4... | collective-permute-start | bytes 344072 | tf_op jit(solution)/shard_map/ppermute | solution.py:179
  54.7 13.7 %collective-permute-start.6 = (bf16[16,16,896]{2,1,0:T(8,128)(2,1)S(1)}, bf16[16,16,896]{2,1,0:T(8,128)(2,1)S(1)}, u32[]{:S(2)}, u32[]{:S(2)}) collective-permute-start(bf16[16,16,896]{2,1,0:T(8,128)(2,1)S(1)} %get-tuple-element.16), channel_id=1, source_target_pairs={{0,8},{8,0},{1,9},{9,1},{2,10},{10,2},{3,11},{11,3},{4,12},{12,4},... | collective-permute-start | bytes 1376264 | tf_op jit(solution)/shard_map/ppermute | solution.py:184
  56.7 42.9 %all-to-all-start.1 = ((bf16[16,16,896]{2,1,0:T(8,128)(2,1)}), bf16[16,16,896]{2,1,0:T(8,128)(2,1)S(1)}, u32[]{:S(2)}, u32[]{:S(2)}) async-start(bf16[16,16,896]{2,1,0:T(8,128)(2,1)} %get-tuple-element.19), calls=%async_computation.1 | async-start | bytes 917504 | tf_op jit(solution)/shard_map/all_to_all | solution.py:198
  68.6 11.6 %collective-permute-start.7 = (bf16[4,16,896]{2,1,0:T(8,128)(2,1)S(1)}, bf16[4,16,896]{2,1,0:T(8,128)(2,1)S(1)}, u32[]{:S(2)}, u32[]{:S(2)}) collective-permute-start(bf16[4,16,896]{2,1,0:T(8,128)(2,1)S(1)} %get-tuple-element.22), channel_id=1, source_target_pairs={{0,1},{1,2},{2,3},{3,0},{4,5},{5,6},{6,7},{7,4},{8,9},{9,10},{10,1... | collective-permute-start | bytes 344072 | tf_op jit(solution)/shard_map/ppermute | solution.py:184
  72.2 8.2 %collective-permute-start.9 = (bf16[4,16,896]{2,1,0:T(8,128)(2,1)S(1)}, bf16[4,16,896]{2,1,0:T(8,128)(2,1)S(1)}, u32[]{:S(2)}, u32[]{:S(2)}) collective-permute-start(bf16[4,16,896]{2,1,0:T(8,128)(2,1)S(1)} %get-tuple-element.23), channel_id=1, source_target_pairs={{0,2},{1,3},{2,0},{3,1},{4,6},{5,7},{6,4},{7,5},{8,10},{9,11},{10,... | collective-permute-start | bytes 344072 | tf_op jit(solution)/shard_map/ppermute | solution.py:184
  76.8 6.7 %collective-permute-start.8 = (bf16[4,16,896]{2,1,0:T(8,128)(2,1)S(1)}, bf16[4,16,896]{2,1,0:T(8,128)(2,1)S(1)}, u32[]{:S(2)}, u32[]{:S(2)}) collective-permute-start(bf16[4,16,896]{2,1,0:T(8,128)(2,1)S(1)} %get-tuple-element.24), channel_id=1, source_target_pairs={{0,3},{1,0},{2,1},{3,2},{4,7},{5,4},{6,5},{7,6},{8,11},{9,8},{10,9... | collective-permute-start | bytes 344072 | tf_op jit(solution)/shard_map/ppermute | solution.py:184
  83.5 10.8 %collective-permute-start.12 = (f32[16,896]{1,0:T(8,128)S(1)}, f32[16,896]{1,0:T(8,128)S(1)}, u32[]{:S(2)}, u32[]{:S(2)}) collective-permute-start(f32[16,896]{1,0:T(8,128)S(1)} %get-tuple-element.26), channel_id=1, source_target_pairs={{0,256},{128,384},{256,0},{384,128},{1,257},{129,385},{257,1},{385... | collective-permute-start | bytes 172040 | tf_op jit(solution)/shard_map/ppermute | solution.py:184
  88.4 6.1 %collective-permute-start.11 = (f32[16,896]{1,0:T(8,128)S(1)}, f32[16,896]{1,0:T(8,128)S(1)}, u32[]{:S(2)}, u32[]{:S(2)}) collective-permute-start(f32[16,896]{1,0:T(8,128)S(1)} %get-tuple-element.27), channel_id=1, source_target_pairs={{0,384},{128,0},{256,128},{384,256},{1,385},{129,1},{257,129},{385... | collective-permute-start | bytes 172040 | tf_op jit(solution)/shard_map/ppermute | solution.py:184
  91.5 7.3 %collective-permute-start.10 = (f32[16,896]{1,0:T(8,128)S(1)}, f32[16,896]{1,0:T(8,128)S(1)}, u32[]{:S(2)}, u32[]{:S(2)}) collective-permute-start(f32[16,896]{1,0:T(8,128)S(1)} %get-tuple-element.28), channel_id=1, source_target_pairs={{0,128},{128,256},{256,384},{384,0},{1,129},{129,257},{257,385},{3... | collective-permute-start | bytes 172040 | tf_op jit(solution)/shard_map/ppermute | solution.py:184

commit v3 on v2

--- a/solution.py
+++ b/solution.py
@@ -199,7 +199,7 @@
     part = part + around(core_part, "core", 1).astype(jnp.float32)
     part = part.reshape((4, 4) + part.shape[1:])
     part = part[0] + sum(
-        around(part[by].astype(jnp.bfloat16), "y", by).astype(jnp.float32) for by in (1, 3, 2)
+        around(part[by].astype(jnp.bfloat16), "y", by).astype(jnp.float32) for by in (2, 1, 3)
     )
     image_back = jnp.stack([part[0]] + [around(part[by], "x", by) for by in (1, 3, 2)], axis=0)
     return (

time: 101 us -> 102 us (level)
  waiting for transfers between devices: 11.3 us -> 13.1 us
    ppermute x7, waiting for transfers between devices: 7.79 us -> 9.61 us  [around(): return lax.ppermute(value, axis, [(i, (i + by) % n) for i in range(n)])]
where the time goes in v3:
time: 102 us
  starting transfers between devices  78.8 us (77%)
  waiting for transfers between devices  13.1 us (13%)
  Pallas kernels  6.48 us (6%)
  between operations  2.15 us (2%)
    ppermute x6, starting transfers between devices, along_z(): return lax.ppermute(value, LINE, pairs)  36 us
    ppermute x7, starting transfers between devices, around(): return lax.ppermute(value, axis, [(i, (i + by) % n) for i in range(n)])  23.6 us
    all_to_all x1, starting transfers between devices, on_device(): text_back = lax.all_to_all(text_part, LINE, 0, 0)  11.8 us
    ppermute x7, waiting for transfers between devices, around(): return lax.ppermute(value, axis, [(i, (i + by) % n) for i in range(n)])  9.61 us
    all_to_all x1, starting transfers between devices, on_device(): images = lax.all_to_all(sent, PLANE, 0, 0)  7.45 us
    pallas_call x1, Pallas kernels, pair_terms(): pl.pallas_call(pair_kernel, in_specs=[pl.BlockSpec(memory_space=pltpu.SME...  3.69 us
    ppermute x6, waiting for transfers between devices, along_z(): return lax.ppermute(value, LINE, pairs)  3.5 us
  transfers between devices with their start and end apart: 15, of which 6 were waited for; matrix products, arithmetic and copies ran while one was open for 0% of the time, Pallas kernels for 1%

profile of v3, /device:TPU:32, one launch (start us, length us, event | category | flops | bytes accessed | tf_op | source)
XLA Modules:
  0.0 101.6 jit_solution(17280483015384566088)
XLA Ops:
  0.6 0.0 copy-start
  0.6 0.8 copy-done
  1.4 1.1 %shard_map.59 = (bf16[32,16,896]{2,1,0:T(8,128)(2,1)}, f32[12,1152]{1,0:T(8,128)S(1)}, f32[12,1]{1,0:T(8,128)S(1)}) custom-call(bf16[12,1152]{1,0:T(8,128)(2,1)S(1)} %copy-done), custom_call_target="tpu_custom_call" | custom-call | flops 100000 | bytes 1000000 | tf_op jit(solution)/shard_map/pallas_call | solution.py:46
  2.5 0.0 copy-start.1
  2.5 7.5 %all-to-all-start = ((bf16[32,16,896]{2,1,0:T(8,128)(2,1)}), bf16[32,16,896]{2,1,0:T(8,128)(2,1)S(1)}, u32[]{:S(2)}, u32[]{:S(2)}) async-start(bf16[32,16,896]{2,1,0:T(8,128)(2,1)} %get-tuple-element.13), calls=%async_computation | async-start | bytes 1835008 | tf_op jit(solution)/shard_map/all_to_all | solution.py:193
  10.0 0.0 copy-done.1
  10.0 0.1 shard_map.60
  10.1 14.8 %collective-permute-start.2 = (bf16[1,16,896]{2,1,0:T(8,128)(2,1)S(1)}, bf16[1,16,896]{2,1,0:T(8,128)(2,1)S(1)}, u32[]{:S(2)}, u32[]{:S(2)}) collective-permute-start(bf16[1,16,896]{2,1,0:T(8,128)(2,1)S(1)} %get-tuple-element.14), channel_id=1, source_target_pairs={{0,4},{16,20},{32,36},{48,52},{64,68},{80,84},{96,100},{112,116},{... | collective-permute-start | bytes 86024 | tf_op jit(solution)/shard_map/ppermute | solution.py:179
  24.9 1.9 %collective-permute-start.1 = (bf16[1,16,896]{2,1,0:T(8,128)(2,1)S(1)}, bf16[1,16,896]{2,1,0:T(8,128)(2,1)S(1)}, u32[]{:S(2)}, u32[]{:S(2)}) collective-permute-start(bf16[1,16,896]{2,1,0:T(8,128)(2,1)S(1)} %get-tuple-element.14), channel_id=1, source_target_pairs={{0,68},{16,84},{32,100},{48,116},{64,0},{80,16},{96,32},{112,48},{... | collective-permute-start | bytes 86024 | tf_op jit(solution)/shard_map/ppermute | solution.py:179
  26.9 7.8 %collective-permute-start = (bf16[1,16,896]{2,1,0:T(8,128)(2,1)S(1)}, bf16[1,16,896]{2,1,0:T(8,128)(2,1)S(1)}, u32[]{:S(2)}, u32[]{:S(2)}) collective-permute-start(bf16[1,16,896]{2,1,0:T(8,128)(2,1)S(1)} %get-tuple-element.14), channel_id=1, source_target_pairs={{0,64},{16,80},{32,96},{48,112},{64,4},{80,20},{96,36},{112,52},{4... | collective-permute-start | bytes 86024 | tf_op jit(solution)/shard_map/ppermute | solution.py:179
  34.7 2.5 %collective-permute-done = bf16[1,16,896]{2,1,0:T(8,128)(2,1)S(1)} collective-permute-done((bf16[1,16,896]{2,1,0:T(8,128)(2,1)S(1)}, bf16[1,16,896]{2,1,0:T(8,128)(2,1)S(1)}, u32[]{:S(2)}, u32[]{:S(2)}) %collective-permute-start) | collective-permute-done | bytes 28704 | tf_op jit(solution)/shard_map/ppermute | solution.py:179
  37.3 0.0 collective-permute-done.1
  37.3 0.0 collective-permute-done.2
  37.3 4.1 %collective-permute-start.5 = (bf16[4,16,896]{2,1,0:T(8,128)(2,1)S(1)}, bf16[4,16,896]{2,1,0:T(8,128)(2,1)S(1)}, u32[]{:S(2)}, u32[]{:S(2)}) collective-permute-start(bf16[4,16,896]{2,1,0:T(8,128)(2,1)S(1)} %constant_dynamic-update-slice_fusion.refs_0_), channel_id=1, source_target_pairs={{0,32},{16,116},{32,64},{48,16},{64,96},{80,48},{96,4},{112,80},{4... | collective-permute-start | bytes 344072 | tf_op jit(solution)/shard_map/ppermute | solution.py:179
  41.4 2.3 %collective-permute-start.4 = (bf16[4,16,896]{2,1,0:T(8,128)(2,1)S(1)}, bf16[4,16,896]{2,1,0:T(8,128)(2,1)S(1)}, u32[]{:S(2)}, u32[]{:S(2)}) collective-permute-start(bf16[4,16,896]{2,1,0:T(8,128)(2,1)S(1)} %constant_dynamic-update-slice_fusion.refs_0_), channel_id=1, source_target_pairs={{0,116},{16,0},{32,16},{48,32},{64,48},{80,64},{96,80},{112,96},{4... | collective-permute-start | bytes 344072 | tf_op jit(solution)/shard_map/ppermute | solution.py:179
  43.8 4.9 %collective-permute-start.3 = (bf16[4,16,896]{2,1,0:T(8,128)(2,1)S(1)}, bf16[4,16,896]{2,1,0:T(8,128)(2,1)S(1)}, u32[]{:S(2)}, u32[]{:S(2)}) collective-permute-start(bf16[4,16,896]{2,1,0:T(8,128)(2,1)S(1)} %constant_dynamic-update-slice_fusion.refs_0_), channel_id=1, source_target_pairs={{0,16},{16,32},{32,48},{48,64},{64,80},{80,96},{96,112},{112,4},{4... | collective-permute-start | bytes 344072 | tf_op jit(solution)/shard_map/ppermute | solution.py:179
  50.0 0.1 pad_add_fusion.place_ref
  50.1 0.0 collective-permute-done.5.refs_3_
  50.1 0.0 collective-permute-done.4.refs_2_
  50.1 1.0 collective-permute-done.3.refs_1_
  51.0 0.0 all-to-all-done.images_ref
  51.1 3.7 %shard_map.61 = (bf16[16,16,896]{2,1,0:T(8,128)(2,1)S(1)}, f32[16,16,896]{2,1,0:T(8,128)S(1)}, bf16[16,16,896]{2,1,0:T(8,128)(2,1)}) custom-call(f32[1]{0:T(128)S(6)} %copy.9.temp_ref, f32[1]{0:T(128)S(6)} %copy.10.bias_ref, s32[2]{0:T(128)S(1)} %pad_add_fusion.place_ref, bf16[32,16,896]{2,1,0:T(8,128)(2,1)S(1)} %all-to-all-done.images_ref, ...), custom_call_target="tpu_custom_call" | custom-call | flops 900000000 | bytes 4000000 | tf_op jit(solution)/shard_map/pallas_call | solution.py:124
  54.7 1.9 %collective-permute-start.6 = (bf16[16,16,896]{2,1,0:T(8,128)(2,1)S(1)}, bf16[16,16,896]{2,1,0:T(8,128)(2,1)S(1)}, u32[]{:S(2)}, u32[]{:S(2)}) collective-permute-start(bf16[16,16,896]{2,1,0:T(8,128)(2,1)S(1)} %get-tuple-element.16), channel_id=1, source_target_pairs={{0,8},{8,0},{1,9},{9,1},{2,10},{10,2},{3,11},{11,3},{4,12},{12,4},... | collective-permute-start | bytes 1376264 | tf_op jit(solution)/shard_map/ppermute | solution.py:184
  56.7 11.8 %all-to-all-start.1 = ((bf16[16,16,896]{2,1,0:T(8,128)(2,1)}), bf16[16,16,896]{2,1,0:T(8,128)(2,1)S(1)}, u32[]{:S(2)}, u32[]{:S(2)}) async-start(bf16[16,16,896]{2,1,0:T(8,128)(2,1)} %get-tuple-element.19), calls=%async_computation.1 | async-start | bytes 917504 | tf_op jit(solution)/shard_map/all_to_all | solution.py:198
  68.5 0.0 collective-permute-done.6
  68.5 0.1 fusion
  68.6 5.1 %collective-permute-start.7 = (bf16[4,16,896]{2,1,0:T(8,128)(2,1)S(1)}, bf16[4,16,896]{2,1,0:T(8,128)(2,1)S(1)}, u32[]{:S(2)}, u32[]{:S(2)}) collective-permute-start(bf16[4,16,896]{2,1,0:T(8,128)(2,1)S(1)} %get-tuple-element.22), channel_id=1, source_target_pairs={{0,2},{1,3},{2,0},{3,1},{4,6},{5,7},{6,4},{7,5},{8,10},{9,11},{10,... | collective-permute-start | bytes 344072 | tf_op jit(solution)/shard_map/ppermute | solution.py:184
  73.7 3.1 %collective-permute-start.9 = (bf16[4,16,896]{2,1,0:T(8,128)(2,1)S(1)}, bf16[4,16,896]{2,1,0:T(8,128)(2,1)S(1)}, u32[]{:S(2)}, u32[]{:S(2)}) collective-permute-start(bf16[4,16,896]{2,1,0:T(8,128)(2,1)S(1)} %get-tuple-element.23), channel_id=1, source_target_pairs={{0,3},{1,0},{2,1},{3,2},{4,7},{5,4},{6,5},{7,6},{8,11},{9,8},{10,9... | collective-permute-start | bytes 344072 | tf_op jit(solution)/shard_map/ppermute | solution.py:184
  76.8 2.8 %collective-permute-start.8 = (bf16[4,16,896]{2,1,0:T(8,128)(2,1)S(1)}, bf16[4,16,896]{2,1,0:T(8,128)(2,1)S(1)}, u32[]{:S(2)}, u32[]{:S(2)}) collective-permute-start(bf16[4,16,896]{2,1,0:T(8,128)(2,1)S(1)} %get-tuple-element.24), channel_id=1, source_target_pairs={{0,1},{1,2},{2,3},{3,0},{4,5},{5,6},{6,7},{7,4},{8,9},{9,10},{10,1... | collective-permute-start | bytes 344072 | tf_op jit(solution)/shard_map/ppermute | solution.py:184
  79.6 0.0 collective-permute-done.7
  79.6 0.8 collective-permute-done.9
  80.4 4.3 %collective-permute-done.8 = bf16[4,16,896]{2,1,0:T(8,128)(2,1)S(1)} collective-permute-done((bf16[4,16,896]{2,1,0:T(8,128)(2,1)S(1)}, bf16[4,16,896]{2,1,0:T(8,128)(2,1)S(1)}, u32[]{:S(2)}, u32[]{:S(2)}) %collective-permute-start.8) | collective-permute-done | bytes 114720 | tf_op jit(solution)/shard_map/ppermute | solution.py:184
  84.8 4.9 %collective-permute-start.12 = (f32[16,896]{1,0:T(8,128)S(1)}, f32[16,896]{1,0:T(8,128)S(1)}, u32[]{:S(2)}, u32[]{:S(2)}) collective-permute-start(f32[16,896]{1,0:T(8,128)S(1)} %get-tuple-element.26), channel_id=1, source_target_pairs={{0,256},{128,384},{256,0},{384,128},{1,257},{129,385},{257,1},{385... | collective-permute-start | bytes 172040 | tf_op jit(solution)/shard_map/ppermute | solution.py:184
  89.6 3.1 %collective-permute-start.11 = (f32[16,896]{1,0:T(8,128)S(1)}, f32[16,896]{1,0:T(8,128)S(1)}, u32[]{:S(2)}, u32[]{:S(2)}) collective-permute-start(f32[16,896]{1,0:T(8,128)S(1)} %get-tuple-element.27), channel_id=1, source_target_pairs={{0,384},{128,0},{256,128},{384,256},{1,385},{129,1},{257,129},{385... | collective-permute-start | bytes 172040 | tf_op jit(solution)/shard_map/ppermute | solution.py:184
  92.7 2.8 %collective-permute-start.10 = (f32[16,896]{1,0:T(8,128)S(1)}, f32[16,896]{1,0:T(8,128)S(1)}, u32[]{:S(2)}, u32[]{:S(2)}) collective-permute-start(f32[16,896]{1,0:T(8,128)S(1)} %get-tuple-element.28), channel_id=1, source_target_pairs={{0,128},{128,256},{256,384},{384,0},{1,129},{129,257},{257,385},{3... | collective-permute-start | bytes 172040 | tf_op jit(solution)/shard_map/ppermute | solution.py:184
  95.5 0.0 collective-permute-done.12
  95.5 0.2 collective-permute-done.11
  95.7 4.3 %collective-permute-done.10 = f32[16,896]{1,0:T(8,128)S(1)} collective-permute-done((f32[16,896]{1,0:T(8,128)S(1)}, f32[16,896]{1,0:T(8,128)S(1)}, u32[]{:S(2)}, u32[]{:S(2)}) %collective-permute-start.10) | collective-permute-done | bytes 57376 | tf_op jit(solution)/shard_map/ppermute | solution.py:184
  100.0 0.7 shard_map.62
  100.8 0.0 all-to-all-done.1.refs_0_
  100.8 0.8 shard_map.63
  (8 shorter events, 0.1 us)
Async XLA Ops:
  0.6 0.8 copy-start
  2.5 7.5 %copy-start.1 = (bf16[12,1152]{1,0:T(8,128)(2,1)S(1)}, bf16[12,1152]{1,0:T(8,128)(2,1)}, u32[]{:S(2)}) copy-start(bf16[12,1152]{1,0:T(8,128)(2,1)} %emb_ref.3) | copy-start | bytes 82948
  2.5 48.5 %all-to-all-start = ((bf16[32,16,896]{2,1,0:T(8,128)(2,1)}), bf16[32,16,896]{2,1,0:T(8,128)(2,1)S(1)}, u32[]{:S(2)}, u32[]{:S(2)}) async-start(bf16[32,16,896]{2,1,0:T(8,128)(2,1)} %get-tuple-element.13), calls=%async_computation | async-start | bytes 1835008 | tf_op jit(solution)/shard_map/all_to_all | solution.py:193
  10.1 27.2 %collective-permute-start.2 = (bf16[1,16,896]{2,1,0:T(8,128)(2,1)S(1)}, bf16[1,16,896]{2,1,0:T(8,128)(2,1)S(1)}, u32[]{:S(2)}, u32[]{:S(2)}) collective-permute-start(bf16[1,16,896]{2,1,0:T(8,128)(2,1)S(1)} %get-tuple-element.14), channel_id=1, source_target_pairs={{0,4},{16,20},{32,36},{48,52},{64,68},{80,84},{96,100},{112,116},{... | collective-permute-start | bytes 86024 | tf_op jit(solution)/shard_map/ppermute | solution.py:179
  24.9 12.3 %collective-permute-start.1 = (bf16[1,16,896]{2,1,0:T(8,128)(2,1)S(1)}, bf16[1,16,896]{2,1,0:T(8,128)(2,1)S(1)}, u32[]{:S(2)}, u32[]{:S(2)}) collective-permute-start(bf16[1,16,896]{2,1,0:T(8,128)(2,1)S(1)} %get-tuple-element.14), channel_id=1, source_target_pairs={{0,68},{16,84},{32,100},{48,116},{64,0},{80,16},{96,32},{112,48},{... | collective-permute-start | bytes 86024 | tf_op jit(solution)/shard_map/ppermute | solution.py:179
  26.9 10.4 %collective-permute-start = (bf16[1,16,896]{2,1,0:T(8,128)(2,1)S(1)}, bf16[1,16,896]{2,1,0:T(8,128)(2,1)S(1)}, u32[]{:S(2)}, u32[]{:S(2)}) collective-permute-start(bf16[1,16,896]{2,1,0:T(8,128)(2,1)S(1)} %get-tuple-element.14), channel_id=1, source_target_pairs={{0,64},{16,80},{32,96},{48,112},{64,4},{80,20},{96,36},{112,52},{4... | collective-permute-start | bytes 86024 | tf_op jit(solution)/shard_map/ppermute | solution.py:179
  37.3 12.8 %collective-permute-start.5 = (bf16[4,16,896]{2,1,0:T(8,128)(2,1)S(1)}, bf16[4,16,896]{2,1,0:T(8,128)(2,1)S(1)}, u32[]{:S(2)}, u32[]{:S(2)}) collective-permute-start(bf16[4,16,896]{2,1,0:T(8,128)(2,1)S(1)} %constant_dynamic-update-slice_fusion.refs_0_), channel_id=1, source_target_pairs={{0,32},{16,116},{32,64},{48,16},{64,96},{80,48},{96,4},{112,80},{4... | collective-permute-start | bytes 344072 | tf_op jit(solution)/shard_map/ppermute | solution.py:179
  41.4 8.7 %collective-permute-start.4 = (bf16[4,16,896]{2,1,0:T(8,128)(2,1)S(1)}, bf16[4,16,896]{2,1,0:T(8,128)(2,1)S(1)}, u32[]{:S(2)}, u32[]{:S(2)}) collective-permute-start(bf16[4,16,896]{2,1,0:T(8,128)(2,1)S(1)} %constant_dynamic-update-slice_fusion.refs_0_), channel_id=1, source_target_pairs={{0,116},{16,0},{32,16},{48,32},{64,48},{80,64},{96,80},{112,96},{4... | collective-permute-start | bytes 344072 | tf_op jit(solution)/shard_map/ppermute | solution.py:179
  43.8 7.3 %collective-permute-start.3 = (bf16[4,16,896]{2,1,0:T(8,128)(2,1)S(1)}, bf16[4,16,896]{2,1,0:T(8,128)(2,1)S(1)}, u32[]{:S(2)}, u32[]{:S(2)}) collective-permute-start(bf16[4,16,896]{2,1,0:T(8,128)(2,1)S(1)} %constant_dynamic-update-slice_fusion.refs_0_), channel_id=1, source_target_pairs={{0,16},{16,32},{32,48},{48,64},{64,80},{80,96},{96,112},{112,4},{4... | collective-permute-start | bytes 344072 | tf_op jit(solution)/shard_map/ppermute | solution.py:179
  54.7 13.7 %collective-permute-start.6 = (bf16[16,16,896]{2,1,0:T(8,128)(2,1)S(1)}, bf16[16,16,896]{2,1,0:T(8,128)(2,1)S(1)}, u32[]{:S(2)}, u32[]{:S(2)}) collective-permute-start(bf16[16,16,896]{2,1,0:T(8,128)(2,1)S(1)} %get-tuple-element.16), channel_id=1, source_target_pairs={{0,8},{8,0},{1,9},{9,1},{2,10},{10,2},{3,11},{11,3},{4,12},{12,4},... | collective-permute-start | bytes 1376264 | tf_op jit(solution)/shard_map/ppermute | solution.py:184
  56.7 44.1 %all-to-all-start.1 = ((bf16[16,16,896]{2,1,0:T(8,128)(2,1)}), bf16[16,16,896]{2,1,0:T(8,128)(2,1)S(1)}, u32[]{:S(2)}, u32[]{:S(2)}) async-start(bf16[16,16,896]{2,1,0:T(8,128)(2,1)} %get-tuple-element.19), calls=%async_computation.1 | async-start | bytes 917504 | tf_op jit(solution)/shard_map/all_to_all | solution.py:198
  68.6 10.9 %collective-permute-start.7 = (bf16[4,16,896]{2,1,0:T(8,128)(2,1)S(1)}, bf16[4,16,896]{2,1,0:T(8,128)(2,1)S(1)}, u32[]{:S(2)}, u32[]{:S(2)}) collective-permute-start(bf16[4,16,896]{2,1,0:T(8,128)(2,1)S(1)} %get-tuple-element.22), channel_id=1, source_target_pairs={{0,2},{1,3},{2,0},{3,1},{4,6},{5,7},{6,4},{7,5},{8,10},{9,11},{10,... | collective-permute-start | bytes 344072 | tf_op jit(solution)/shard_map/ppermute | solution.py:184
  73.7 6.7 %collective-permute-start.9 = (bf16[4,16,896]{2,1,0:T(8,128)(2,1)S(1)}, bf16[4,16,896]{2,1,0:T(8,128)(2,1)S(1)}, u32[]{:S(2)}, u32[]{:S(2)}) collective-permute-start(bf16[4,16,896]{2,1,0:T(8,128)(2,1)S(1)} %get-tuple-element.23), channel_id=1, source_target_pairs={{0,3},{1,0},{2,1},{3,2},{4,7},{5,4},{6,5},{7,6},{8,11},{9,8},{10,9... | collective-permute-start | bytes 344072 | tf_op jit(solution)/shard_map/ppermute | solution.py:184
  76.8 7.9 %collective-permute-start.8 = (bf16[4,16,896]{2,1,0:T(8,128)(2,1)S(1)}, bf16[4,16,896]{2,1,0:T(8,128)(2,1)S(1)}, u32[]{:S(2)}, u32[]{:S(2)}) collective-permute-start(bf16[4,16,896]{2,1,0:T(8,128)(2,1)S(1)} %get-tuple-element.24), channel_id=1, source_target_pairs={{0,1},{1,2},{2,3},{3,0},{4,5},{5,6},{6,7},{7,4},{8,9},{9,10},{10,1... | collective-permute-start | bytes 344072 | tf_op jit(solution)/shard_map/ppermute | solution.py:184
  84.8 10.8 %collective-permute-start.12 = (f32[16,896]{1,0:T(8,128)S(1)}, f32[16,896]{1,0:T(8,128)S(1)}, u32[]{:S(2)}, u32[]{:S(2)}) collective-permute-start(f32[16,896]{1,0:T(8,128)S(1)} %get-tuple-element.26), channel_id=1, source_target_pairs={{0,256},{128,384},{256,0},{384,128},{1,257},{129,385},{257,1},{385... | collective-permute-start | bytes 172040 | tf_op jit(solution)/shard_map/ppermute | solution.py:184
  89.6 6.1 %collective-permute-start.11 = (f32[16,896]{1,0:T(8,128)S(1)}, f32[16,896]{1,0:T(8,128)S(1)}, u32[]{:S(2)}, u32[]{:S(2)}) collective-permute-start(f32[16,896]{1,0:T(8,128)S(1)} %get-tuple-element.27), channel_id=1, source_target_pairs={{0,384},{128,0},{256,128},{384,256},{1,385},{129,1},{257,129},{385... | collective-permute-start | bytes 172040 | tf_op jit(solution)/shard_map/ppermute | solution.py:184
  92.7 7.3 %collective-permute-start.10 = (f32[16,896]{1,0:T(8,128)S(1)}, f32[16,896]{1,0:T(8,128)S(1)}, u32[]{:S(2)}, u32[]{:S(2)}) collective-permute-start(f32[16,896]{1,0:T(8,128)S(1)} %get-tuple-element.28), channel_id=1, source_target_pairs={{0,128},{128,256},{256,384},{384,0},{1,129},{129,257},{257,385},{3... | collective-permute-start | bytes 172040 | tf_op jit(solution)/shard_map/ppermute | solution.py:184
